TPU v7x, 32 devices: a whole 2x2x4 slice. The times are simulated.
32 devices in a mesh: req: 8 (over z, x), tp: 4 (over y, core).
Axes of the slice: x: 2, y: 2, z: 4, core: 2. Of those that a mesh axis runs over, the one named last changes fastest.
Arguments:
- tokens: bfloat16 [8192, 1280], P('req'), may hold values from -14 to 14
- segments: int32 [8192], P('req'), may hold values from 0 to 6, never falling along the last dimension, each value on 1 to 2048 neighbouring positions
- attend_gain: bfloat16 [1280], replicated, may hold values from 0.25 to 1.75
- attend_weight: bfloat16 [1280, 3, 1280], P(None, None, 'tp'), may hold values from -1 to 1
- output_weight: bfloat16 [1280, 1280], P('tp'), may hold values from -0.15625 to 0.15625
- mixer_gain: bfloat16 [1280], replicated, may hold values from 0.25 to 1.75
- expand_weight: bfloat16 [1280, 5120], P(None, 'tp'), may hold values from -0.15625 to 0.15625
- reduce_weight: bfloat16 [5120, 1280], P('tp'), may hold values from -0.078125 to 0.078125
- output_gain: bfloat16 [1280], replicated, may hold values from 0.25 to 1.75
- merge_weight: bfloat16 [5120, 1280], P(None, 'tp'), may hold values from -0.078125 to 0.078125
- merge_index: int32 [2048, 4], P('req'), may hold values from 0 to 8191, as said below
- owners: int32 [2048, 1], P('req'), may hold values from 0 to 7; in each aligned block of 256 rows (0 to 255, 256 to 511, ...) at most 64 rows name the same one
Outputs:
- owned: bfloat16 [8, 8, 64, 1280], P('req', None, None, 'tp')
Inputs may be any that keep to these rules, and one draw needn't show every extreme that they name: segments never fall along the tokens; every image has at most 2048 tokens. `merge_index`: merged rows 256 * j to 256 * (j + 1) - 1 name the tokens 1024 * j to 1024 * (j + 1) - 1, each exactly once. `owners`: within the rows of one index of req each owner is named at most 64 times.
All inputs are finite; a program needn't handle non-finite values.
Results may differ from a plain program's by a relative error of at most 0.014.
Values may be sent and summed in bfloat16 or wider, within the bound.
No kernel may reach another device: no remote copies, remote signals or barrier semaphores. Data moves between devices by JAX's collectives and lax.ppermute only.
A program may use at most 128 MiB of HBM per device.

v0:
```python
import functools
import math

import jax
import jax.numpy as jnp
from jax import lax
from jax.experimental import pallas as pl
from jax.experimental.pallas import tpu as pltpu
from jax.sharding import PartitionSpec as P

HD = 80
TILE = 512
MASKED = -1e30
START = -1e28
FACTOR = 1.0 / math.sqrt(HD)
MIB = 1 << 20


def swap(block, axis, flip):
    return lax.ppermute(block, axis, [(i, i ^ flip) for i in range(lax.axis_size(axis))])


def shifted(block, axis, distance):
    devices = range(lax.axis_size(axis))
    route = [(i - distance, i) for i in devices if i - distance in devices]
    return lax.ppermute(block, axis, route)


def normalized(stream, gain):
    center = jnp.mean(stream, axis=-1, keepdims=True)
    moved = stream - center
    spread = jnp.mean(moved * moved, axis=-1, keepdims=True)
    return (moved * lax.rsqrt(spread + 1e-06) * gain).astype(jnp.bfloat16)


def dot(a, b, contract):
    return lax.dot_general(a, b, (contract, ((), ())), preferred_element_type=jnp.float32)


NN = ((1,), (0,))
NT = ((1,), (1,))


def vmem(limit):
    return pltpu.CompilerParams(vmem_limit_bytes=limit * MIB)


def project_kernel(par_ref, x_ref, gain_ref, w_ref, kv_keep, kv_send, q_keep, q_send):
    par = par_ref[0]
    half = w_ref.shape[2]
    rows = normalized(x_ref[...].astype(jnp.float32), gain_ref[...])
    for which, kv, q in ((par, kv_keep, q_keep), (1 - par, kv_send, q_send)):
        for part in (1, 2):
            out = dot(w_ref[part, which], rows, NT).astype(jnp.bfloat16)
            kv[(part - 1) * half : part * half, :] = out
        q[...] = dot(w_ref[0, which], rows, NT).astype(jnp.bfloat16)


def project(par, tokens, gain, weight):
    rows, width = tokens.shape
    half = weight.shape[2]
    step = 256
    shapes = [(2 * half, rows), (2 * half, rows), (half, rows), (half, rows)]
    return pl.pallas_call(
        project_kernel,
        grid_spec=pltpu.PrefetchScalarGridSpec(
            num_scalar_prefetch=1,
            grid=(rows // step,),
            in_specs=[
                pl.BlockSpec((step, width), lambda i, s: (i, 0)),
                pl.BlockSpec((1, width), lambda i, s: (0, 0)),
                pl.BlockSpec(weight.shape, lambda i, s: (0, 0, 0, 0)),
            ],
            out_specs=[pl.BlockSpec((s[0], step), lambda i, s: (0, i)) for s in shapes],
        ),
        out_shape=[jax.ShapeDtypeStruct(s, jnp.bfloat16) for s in shapes],
        compiler_params=vmem(32),
        name="project",
    )(par, tokens, gain, weight)


def attend_kernel(blocks, base, first, last, meta, *refs):
    q_refs, refs = refs[:2], refs[2:]
    kv_refs, refs = refs[:blocks], refs[blocks:]
    q_segment, k_segment, refs = refs[0], refs[1], refs[2:]
    if first:
        acc_out, ml_out, refs = refs[0], refs[1], refs[2:]
    else:
        acc_in, ml_in, ctx_out, refs = refs[0], refs[1], refs[2], refs[3:]
    keys, values, columns, acc, ml = refs
    heads = 2
    tiles_of = kv_refs[0].shape[1] // TILE
    tiles = blocks * tiles_of
    j = pl.program_id(0)

    @pl.when(j == 0)
    def _():
        for b in range(blocks):
            for t in range(tiles_of):
                at = slice(t * TILE, (t + 1) * TILE)
                for h in range(heads):
                    block = kv_refs[b][h * HD : (h + 1) * HD, at].astype(jnp.float32)
                    keys[b * tiles_of + t, h] = jnp.transpose(block).astype(jnp.bfloat16)
                    values[b * tiles_of + t, h] = kv_refs[b][
                        (heads + h) * HD : (heads + h + 1) * HD, at
                    ]
                row = jnp.broadcast_to(k_segment[b : b + 1, at], (128, TILE))
                columns[b * tiles_of + t] = jnp.transpose(row)

    if first:
        acc[...] = jnp.zeros_like(acc)
        ml[0:2, :] = jnp.full((2, TILE), START, jnp.float32)
        ml[2:4, :] = jnp.zeros((2, TILE), jnp.float32)
    else:
        acc[...] = acc_in[0]
        ml[...] = ml_in[0]

    queries = jnp.where(j < 2, q_refs[0][...], q_refs[1][...])
    q_low, q_high = meta[2 + 2 * j], meta[3 + 2 * j]
    q_row = q_segment[0]

    def update(t, masked):
        if masked:
            column = columns[t]
            matches = jnp.concatenate([column] * (TILE // 128), axis=1) == q_row
        for h in range(heads):
            scores = dot(keys[t, h], queries[h * HD : (h + 1) * HD, :], NN)
            if masked:
                scores = jnp.where(matches, scores, MASKED)
            old = ml[h : h + 1, :]
            new = jnp.maximum(old, jnp.max(scores, axis=0, keepdims=True))
            probs = jnp.exp((scores - new) * FACTOR)
            shrink = jnp.exp((old - new) * FACTOR)
            ml[h : h + 1, :] = new
            ml[2 + h : 3 + h, :] = ml[2 + h : 3 + h, :] * shrink + jnp.sum(
                probs, axis=0, keepdims=True
            )
            acc[h * HD : (h + 1) * HD, :] = acc[h * HD : (h + 1) * HD, :] * shrink + dot(
                values[t, h], probs.astype(jnp.bfloat16), NN
            )

    def visit(t, carry):
        at = 10 + 2 * (base * tiles_of + t)
        k_low, k_high = meta[at], meta[at + 1]
        touches = (k_high >= q_low) & (k_low <= q_high)
        whole = (k_low == k_high) & (q_low == q_high)

        @pl.when(touches & whole)
        def _():
            update(t, False)

        @pl.when(touches & jnp.logical_not(whole))
        def _():
            update(t, True)

        return carry

    lax.fori_loop(0, tiles, visit, 0)
    if first:
        acc_out[0] = acc[...]
        ml_out[0] = ml[...]
    else:
        for h in range(heads):
            at = slice(h * HD, (h + 1) * HD)
            ctx_out[0, at, :] = (acc[at, :] / ml[2 + h : 3 + h, :]).astype(jnp.bfloat16)


def attend(meta, q_own, q_peer, key_values, q_segment, k_segment, base, state=None):
    half, rows = q_own.shape
    blocks = len(key_values)
    tiles = blocks * rows // TILE
    q_spec = pl.BlockSpec((half, TILE), lambda j, s: (0, (j % 2) ^ s[1]))
    whole = lambda a: pl.BlockSpec(a.shape, lambda j, s: (0,) * a.ndim)
    acc_spec = pl.BlockSpec((1, half, TILE), lambda j, s: (j, 0, 0))
    ml_spec = pl.BlockSpec((1, 4, TILE), lambda j, s: (j, 0, 0))
    in_specs = [q_spec, q_spec] + [whole(kv) for kv in key_values]
    in_specs += [pl.BlockSpec((1, 1, TILE), lambda j, s: (j, 0, 0)), whole(k_segment)]
    operands = [q_own, q_peer, *key_values, q_segment, k_segment]
    if state is None:
        out_specs = [acc_spec, ml_spec]
        out_shape = [
            jax.ShapeDtypeStruct((4, half, TILE), jnp.float32),
            jax.ShapeDtypeStruct((4, 4, TILE), jnp.float32),
        ]
    else:
        in_specs += [acc_spec, ml_spec]
        operands += list(state)
        out_specs = acc_spec
        out_shape = jax.ShapeDtypeStruct((4, half, TILE), jnp.bfloat16)
    return pl.pallas_call(
        functools.partial(attend_kernel, blocks, base, state is None, state is not None),
        grid_spec=pltpu.PrefetchScalarGridSpec(
            num_scalar_prefetch=1,
            grid=(4,),
            in_specs=in_specs,
            out_specs=out_specs,
            scratch_shapes=[
                pltpu.VMEM((tiles, 2, TILE, HD), jnp.bfloat16),
                pltpu.VMEM((tiles, 2, HD, TILE), jnp.bfloat16),
                pltpu.VMEM((tiles, TILE, 128), jnp.float32),
                pltpu.VMEM((half, TILE), jnp.float32),
                pltpu.VMEM((4, TILE), jnp.float32),
            ],
        ),
        out_shape=out_shape,
        compiler_params=vmem(40),
        cost_estimate=pl.CostEstimate(
            flops=8_000_000_000, bytes_accessed=8_000_000, transcendentals=8_000_000
        ),
        name="attend_local" if state is None else "attend_far",
    )(meta, *operands)


def mixer_kernel(place, *refs):
    pieces, refs = refs[:8], refs[8:]
    x_ref, gain_ref, refs = refs[0], refs[1], refs[2:]
    wo_hbm, refs = refs[:4], refs[4:]
    (we_own, we_other, wr_own, wr_other, sent, kept, refs) = (*refs[:6], refs[6:])
    context, wo, we, wr, sems = refs
    par = place[0]
    half = pieces[0].shape[0]
    copies = []
    for t in range(4):
        copies.append(pltpu.make_async_copy(wo_hbm[t], wo.at[t], sems.at[t]))
    copies.append(pltpu.make_async_copy(we_own, we.at[0], sems.at[4]))
    copies.append(pltpu.make_async_copy(we_other, we.at[1], sems.at[5]))
    copies.append(pltpu.make_async_copy(wr_own, wr.at[0], sems.at[6]))
    copies.append(pltpu.make_async_copy(wr_other, wr.at[1], sems.at[7]))
    for copy in copies:
        copy.start()
    total = x_ref[...].astype(jnp.float32)
    for t in range(4):
        copies[t].wait()
        for h in range(2):
            piece = jnp.transpose(pieces[2 * t + h][...].astype(jnp.float32))
            total += dot(piece.astype(jnp.bfloat16), wo[t, par ^ h], NN)
    rows = normalized(total, gain_ref[...])
    for s in range(2):
        copies[4 + s].wait()
        copies[6 + s].wait()
        hidden = we.shape[2]
        step = 256
        for n in range(hidden // step):
            at = slice(n * step, (n + 1) * step)
            inner = dot(rows, we[s, :, at], NN)
            grown = 0.5 * inner * (1.0 + lax.erf(inner * (1.0 / math.sqrt(2.0))))
            context[:, s * hidden + n * step : s * hidden + (n + 1) * step] = grown.astype(
                jnp.bfloat16
            )
    hidden = we.shape[2]
    out = dot(context[:, :hidden], wr[0], NN) + dot(context[:, hidden:], wr[1], NN)
    sent[...] = out.astype(jnp.bfloat16)
    kept[...] = total + out


def mixer(place, pieces, tokens, gain, wo, weights, chunk, chunk_rows):
    half = pieces[0].shape[0]
    width = tokens.shape[1]
    per_core = pieces[0].shape[1]
    chunks = per_core // chunk_rows
    hidden = weights[0].shape[1]
    piece_spec = pl.BlockSpec((half, chunk_rows), lambda i, s: (0, chunk))
    any_spec = pl.BlockSpec(memory_space=pl.ANY)
    out_spec = pl.BlockSpec((chunk_rows, width), lambda i, s: (0, 0))
    return pl.pallas_call(
        mixer_kernel,
        grid_spec=pltpu.PrefetchScalarGridSpec(
            num_scalar_prefetch=1,
            grid=(1,),
            in_specs=[piece_spec] * 8
            + [
                pl.BlockSpec((chunk_rows, width), lambda i, s: (s[1] * chunks + chunk, 0)),
                pl.BlockSpec((1, width), lambda i, s: (0, 0)),
            ]
            + [any_spec] * 8,
            out_specs=[out_spec, out_spec],
            scratch_shapes=[
                pltpu.VMEM((chunk_rows, 2 * hidden), jnp.bfloat16),
                pltpu.VMEM((4,) + wo[0].shape, jnp.bfloat16),
                pltpu.VMEM((2,) + weights[0].shape, jnp.bfloat16),
                pltpu.VMEM((2,) + weights[2].shape, jnp.bfloat16),
                pltpu.SemaphoreType.DMA((8,)),
            ],
        ),
        out_shape=[
            jax.ShapeDtypeStruct((chunk_rows, width), jnp.bfloat16),
            jax.ShapeDtypeStruct((chunk_rows, width), jnp.float32),
        ],
        compiler_params=vmem(48),
        cost_estimate=pl.CostEstimate(
            flops=5_000_000_000, bytes_accessed=20_000_000, transcendentals=0
        ),
        name="mixer",
    )(place, *pieces, tokens, gain, *wo, *weights)


def one_hot_rows(index_ref, k, first, rows):
    column = jnp.transpose(jnp.broadcast_to(index_ref[k : k + 1, :], (128, index_ref.shape[1])))
    lanes = lax.broadcasted_iota(jnp.int32, (1, 128), 1)
    parts = [column == lanes + (first + 128 * n) for n in range(rows // 128)]
    return jnp.concatenate(parts, axis=1).astype(jnp.float32).astype(jnp.bfloat16)


def gather_kernel(place, index_ref, kept, received, gain_ref, merged):
    rows = kept.shape[0]
    final = normalized(kept[...] + received[...].astype(jnp.float32), gain_ref[...])
    for k in range(4):
        merged[k] = dot(one_hot_rows(index_ref, k, place[2], rows), final, NN).astype(jnp.bfloat16)


def gather(place, index, kept, received, gain):
    rows, width = kept.shape
    merged_rows = index.shape[1]
    whole = lambda a: pl.BlockSpec(a.shape, lambda i, s: (0,) * a.ndim)
    return pl.pallas_call(
        gather_kernel,
        grid_spec=pltpu.PrefetchScalarGridSpec(
            num_scalar_prefetch=1,
            grid=(1,),
            in_specs=[whole(index), whole(kept), whole(received), whole(gain)],
            out_specs=pl.BlockSpec((4, merged_rows, width), lambda i, s: (0, 0, 0)),
        ),
        out_shape=jax.ShapeDtypeStruct((4, merged_rows, width), jnp.bfloat16),
        compiler_params=vmem(32),
        cost_estimate=pl.CostEstimate(
            flops=1_000_000_000, bytes_accessed=5_000_000, transcendentals=0
        ),
        name="gather",
    )(place, index, kept, received, gain)


def merge_kernel(place, index_ref, kept, received, gain_ref, earlier, w_own, w_other, own, other):
    rows = kept.shape[0]
    width = kept.shape[1]
    final = normalized(kept[...] + received[...].astype(jnp.float32), gain_ref[...])
    own[...] = jnp.zeros_like(own)
    other[...] = jnp.zeros_like(other)
    for k in range(4):
        part = dot(one_hot_rows(index_ref, k, place[3], rows), final, NN)
        part = (part + earlier[k].astype(jnp.float32)).astype(jnp.bfloat16)
        own[...] += dot(part, w_own[:, k * width : (k + 1) * width], NT)
        other[...] += dot(part, w_other[:, k * width : (k + 1) * width], NT)


def merge(place, index, kept, received, gain, earlier, w_own, w_other):
    merged_rows = index.shape[1]
    columns = w_own.shape[0]
    whole = lambda a: pl.BlockSpec(a.shape, lambda i, s: (0,) * a.ndim)
    out_spec = pl.BlockSpec((merged_rows, columns), lambda i, s: (0, 0))
    operands = [index, kept, received, gain, earlier, w_own, w_other]
    return pl.pallas_call(
        merge_kernel,
        grid_spec=pltpu.PrefetchScalarGridSpec(
            num_scalar_prefetch=1,
            grid=(1,),
            in_specs=[whole(a) for a in operands],
            out_specs=[out_spec, out_spec],
        ),
        out_shape=[jax.ShapeDtypeStruct((merged_rows, columns), jnp.float32)] * 2,
        compiler_params=vmem(40),
        cost_estimate=pl.CostEstimate(
            flops=3_000_000_000, bytes_accessed=12_000_000, transcendentals=0
        ),
        name="merge",
    )(place, *operands)


def place_kernel(position, own, received, out):
    feature = (own[...] + received[...]).astype(jnp.bfloat16)
    slots = lax.broadcasted_iota(jnp.int32, (out.shape[0], 1), 0)
    chosen = (slots == position[...]).astype(jnp.float32).astype(jnp.bfloat16)
    out[...] = dot(chosen, feature, NN).astype(jnp.bfloat16)


def body(
    tokens,
    segments,
    attend_gain,
    attend_weight,
    output_weight,
    mixer_gain,
    expand_weight,
    reduce_weight,
    output_gain,
    merge_weight,
    merge_index,
    owners,
):
    rows, width = tokens.shape
    head_width = attend_weight.shape[2]
    half = head_width // 2
    peers = lax.axis_size("req")
    req = lax.axis_index("req")
    par = req % 2
    core = lax.axis_index("tp") % 2

    with jax.named_scope("project"):
        weight = jnp.transpose(attend_weight, (1, 2, 0)).reshape(3, 2, half, width)
        kv_own, kv_send, q_own, q_send = project(
            par.reshape(1), tokens, attend_gain.astype(jnp.float32)[None, :], weight
        )

    with jax.named_scope("exchange_keys"):
        kv_peer = swap(kv_send, "req", 1)
        kv_before = shifted(kv_own, "req", 2)
        kv_after = shifted(kv_own, "req", -2)
        q_peer = swap(q_send, "req", 1)
        kv_before_peer = shifted(kv_peer, "req", 2)
        kv_after_peer = shifted(kv_peer, "req", -2)

    with jax.named_scope("segments"):
        every = lax.all_gather(segments, "req", axis=0, tiled=True)
        every = jnp.pad(every, (2 * rows, 2 * rows), constant_values=-1)
        window = lax.dynamic_slice_in_dim(every, (req - par) * rows, 6 * rows, 0)
        window = window.reshape(3, 2, rows)
        window = jnp.where(par == 0, window, window[:, ::-1])
        key_rows = jnp.concatenate([window[1], window[0], window[2]], axis=0)
        tiles = window[1].reshape(2, rows // TILE, TILE)
        tiles = jnp.where(core == 0, tiles, tiles[:, ::-1]).reshape(4, TILE)
        key_tiles = key_rows.reshape(-1, TILE)
        meta = jnp.concatenate(
            [
                jnp.stack([par, core]),
                tiles[:, :: TILE - 1].reshape(-1),
                key_tiles[:, :: TILE - 1].reshape(-1),
            ]
        )
        q_segment = tiles.astype(jnp.float32)[:, None, :]
        key_rows = key_rows.astype(jnp.float32)

    with jax.named_scope("weights"):
        wo = [output_weight.reshape(2, half, width)]
        wo.append(swap(wo[0], "tp", 1))
        wo.append(swap(wo[0], "tp", 2))
        wo.append(swap(wo[2], "tp", 1))
        expand_other = swap(expand_weight, "tp", 1)
        reduce_other = swap(reduce_weight, "tp", 1)
        merge_own = jnp.transpose(merge_weight)
        merge_other = swap(merge_own, "tp", 1)

    with jax.named_scope("attention"):
        state = attend(meta, q_own, q_peer, [kv_own, kv_peer], q_segment, key_rows[:2], 0)
        context = attend(
            meta,
            q_own,
            q_peer,
            [kv_before, kv_before_peer, kv_after, kv_after_peer],
            q_segment,
            key_rows[2:],
            2,
            state,
        )

    with jax.named_scope("exchange_context"):
        from_peer = swap(context[2:], "req", 1)
        pieces = []
        for source in (context, from_peer):
            pieces.append(
                [
                    source[0],
                    swap(source[1], "tp", 1),
                    swap(source[0], "tp", 2),
                    swap(source[1], "tp", 3),
                ]
            )
        pieces = [pieces[h][t] for t in range(4) for h in range(2)]

    chunk_rows = 256
    per_core = rows // 2
    place = jnp.stack([par, core, core * per_core, core * per_core + chunk_rows])
    with jax.named_scope("mixer"):
        gain = mixer_gain.astype(jnp.float32)[None, :]
        weights = [expand_weight, expand_other, reduce_weight, reduce_other]
        sent, kept, received = [], [], []
        for chunk in range(2):
            s, k = mixer(place, pieces, tokens, gain, wo, weights, chunk, chunk_rows)
            kept.append(k)
            received.append(swap(s, "tp", 2))

    with jax.named_scope("merge"):
        index = jnp.transpose(merge_index) - req * rows
        gain = output_gain.astype(jnp.float32)[None, :]
        earlier = gather(place, index, kept[0], received[0], gain)
        own, other = merge(
            place, index, kept[1], received[1], gain, earlier, merge_own, merge_other
        )
        other = swap(other, "tp", 1)

    with jax.named_scope("place"):
        capacity = 2 * merge_index.shape[0] // peers
        target = owners[:, 0]
        choose = (target[:, None] == jnp.arange(peers, dtype=jnp.int32)[None, :]).astype(jnp.int32)
        slot = jnp.sum((jnp.cumsum(choose, axis=0) - 1) * choose, axis=1)
        position = (target * capacity + slot)[None, :]
        columns = own.shape[1]
        outgoing = pl.pallas_call(
            place_kernel,
            out_shape=jax.ShapeDtypeStruct((peers * capacity, columns), jnp.bfloat16),
            name="place",
        )(position, own, other)
        outgoing = outgoing.reshape(peers, capacity, columns)
        arrived = lax.all_to_all(outgoing, "req", split_axis=0, concat_axis=0, tiled=True)
    return arrived.reshape(1, peers, capacity, columns)


def solution(mesh):
    placed = (
        P("req", None),
        P("req"),
        P(),
        P(None, None, "tp"),
        P("tp", None),
        P(),
        P(None, "tp"),
        P("tp", None),
        P(),
        P(None, "tp"),
        P("req", None),
        P("req", None),
    )
    return jax.shard_map(
        body, mesh=mesh, in_specs=placed, out_specs=P("req", None, None, "tp"), check_vma=False
    )
```

profile of v0, /device:TPU:0, one launch (start us, length us, event | category | flops | bytes accessed | tf_op | source)
XLA Modules:
  0.0 231.4 jit_solution(5810285122449617199)
XLA Ops:
  0.0 0.7 reshape.86.gain_ref
  0.7 1.7 copy-done
  2.5 1.7 copy-done.10
  4.1 7.2 %project.1 = (bf16[320,1024]{1,0:T(8,128)(2,1)}, bf16[320,1024]{1,0:T(8,128)(2,1)S(1)}, bf16[160,1024]{1,0:T(8,128)(2,1)S(1)}, bf16[160,1024]{1,0:T(8,128)(2,1)S(1)}) custom-call(s32[1]{0:T(128)} %bitcast.6.par_ref, bf16[1024,1280]{1,0:T(8,128)(2,1)S(1)} %copy-done, f32[1,1280]{1,0:T(1,128)S(1)} %reshape.86.gain_ref, bf16[3,2,160,1280]{3,2,1,0:T(8,128)(2,1)S(1)} %bitcast.44), custom_call_target="tpu_custom_call" | custom-call | tf_op jit(solution)/shard_map/project/project/pallas_call | solution.py:64
  11.4 0.7 copy-done.24
  12.1 2.9 %collective-permute-start = (bf16[160,1024]{1,0:T(8,128)(2,1)S(1)}, bf16[160,1024]{1,0:T(8,128)(2,1)S(1)}, u32[]{:S(2)}, u32[]{:S(2)}) collective-permute-start(bf16[160,1024]{1,0:T(8,128)(2,1)S(1)} %get-tuple-element.18), channel_id=1, source_target_pairs={{0,4},{4,0},{8,12},{12,8},{16,20},{20,16},{24,28},{28,24},{1,5},{5... | collective-permute-start | bytes 983048 | tf_op jit(solution)/shard_map/exchange_keys/ppermute | solution.py:20
  15.1 3.5 %collective-permute-start.1 = (bf16[320,1024]{1,0:T(8,128)(2,1)}, bf16[320,1024]{1,0:T(8,128)(2,1)S(1)}, u32[]{:S(2)}, u32[]{:S(2)}) collective-permute-start(bf16[320,1024]{1,0:T(8,128)(2,1)} %get-tuple-element.19.refs_2_), channel_id=1, source_target_pairs={{0,8},{4,12},{8,16},{12,20},{16,24},{20,28},{1,9},{5,13},{9,17},{1... | collective-permute-start | bytes 1966088 | tf_op jit(solution)/shard_map/exchange_keys/ppermute | solution.py:26
  18.6 0.6 collective-permute-start.2
  19.2 0.5 collective-permute-start.17
  19.7 41.4 %all_gather.3 = s32[8192]{0:T(1024)S(1)} all-gather(s32[1024]{0:T(1024)S(1)} %copy-done.32), channel_id=1, replica_groups=mesh['req'=8,'tp'=4] {'req'}, dimensions={0}, use_global_device_ids=true | all-gather | bytes 36864 | tf_op jit(solution)/shard_map/segments/all_gather | solution.py:412
  61.1 0.3 rev.6
  62.2 0.7 copy-done.27
  62.9 1.3 collective-permute-start.4
  64.2 4.6 %collective-permute-start.3 = (bf16[320,1024]{1,0:T(8,128)(2,1)}, bf16[320,1024]{1,0:T(8,128)(2,1)S(1)}, u32[]{:S(2)}, u32[]{:S(2)}) collective-permute-start(bf16[320,1024]{1,0:T(8,128)(2,1)} %collective-permute-done.2.refs_3_), channel_id=1, source_target_pairs={{0,8},{4,12},{8,16},{12,20},{16,24},{20,28},{1,9},{5,13},{9,17},{1... | collective-permute-start | bytes 1966088 | tf_op jit(solution)/shard_map/exchange_keys/ppermute | solution.py:26
  68.8 0.8 copy-done.22
  69.7 1.3 collective-permute-start.5
  71.0 1.0 copy-done.25
  71.9 1.0 copy-done.28
  72.9 23.4 %attend_local.1 = (f32[4,160,512]{2,1,0:T(8,128)S(1)}, f32[4,4,512]{2,1,0:T(4,128)S(1)}) custom-call(s32[34]{0:T(128)S(1)} %pad_add_fusion.2.meta, bf16[160,1024]{1,0:T(8,128)(2,1)S(1)} %copy-done.25, bf16[160,1024]{1,0:T(8,128)(2,1)S(1)} %copy-done.28, bf16[320,1024]{1,0:T(8,128)(2,1)} %get-tuple-element.19.refs_2_, ...), custom_call_target="tpu_custom_call" | custom-call | flops 8000000000 | bytes 8000000 | tf_op jit(solution)/shard_map/attention/attend_local/pallas_call | solution.py:190
  96.4 1.6 collective-permute-start.14
  98.2 4.2 %attend_far.1 = bf16[4,160,512]{2,1,0:T(8,128)(2,1)S(1)} custom-call(s32[34]{0:T(128)S(1)} %pad_add_fusion.2.meta, bf16[160,1024]{1,0:T(8,128)(2,1)S(1)} %copy-done.26, bf16[160,1024]{1,0:T(8,128)(2,1)S(1)} %copy-done.29, bf16[320,1024]{1,0:T(8,128)(2,1)S(1)} %copy-done.23, bf16[320,1024]{1,0:T(8,128)(2,1)S(1)} %collective-permute-done.3.refs_3_, ...), custom_call_target="tpu_custom_call" | custom-call | flops 8000000000 | bytes 8000000 | tf_op jit(solution)/shard_map/attention/attend_far/pallas_call | solution.py:190
  102.5 0.9 copy-done.4
  103.4 0.3 collective-permute-start.7
  103.7 13.4 %collective-permute-done.14.refs_12_ = bf16[2,160,1280]{2,1,0:T(8,128)(2,1)S(1)} collective-permute-done((bf16[2,160,1280]{2,1,0:T(8,128)(2,1)S(1)}, bf16[2,160,1280]{2,1,0:T(8,128)(2,1)S(1)}, u32[]{:S(2)}, u32[]{:S(2)}) %collective-permute-start.14) | collective-permute-done | bytes 819232 | tf_op jit(solution)/shard_map/weights/ppermute | solution.py:20
  117.1 1.5 collective-permute-start.9
  118.6 0.7 copy-done.13
  119.3 0.9 copy-done.6
  120.2 2.6 %collective-permute-done.9.refs_4_ = bf16[160,512]{1,0:T(8,128)(2,1)S(1)} collective-permute-done((bf16[160,512]{1,0:T(8,128)(2,1)S(1)}, bf16[160,512]{1,0:T(8,128)(2,1)S(1)}, u32[]{:S(2)}, u32[]{:S(2)}) %collective-permute-start.9) | collective-permute-done | bytes 163872 | tf_op jit(solution)/shard_map/exchange_context/ppermute | solution.py:20
  122.9 1.5 collective-permute-start.6
  124.4 6.8 %collective-permute-done.6 = bf16[2,160,512]{2,1,0:T(8,128)(2,1)S(1)} collective-permute-done((bf16[2,160,512]{2,1,0:T(8,128)(2,1)S(1)}, bf16[2,160,512]{2,1,0:T(8,128)(2,1)S(1)}, u32[]{:S(2)}, u32[]{:S(2)}) %collective-permute-start.6) | collective-permute-done | bytes 327712 | tf_op jit(solution)/shard_map/exchange_context/ppermute | solution.py:20
  131.2 0.7 slice_bitcast_fusion
  132.0 5.7 %collective-permute-done.11.refs_6_ = bf16[160,512]{1,0:T(8,128)(2,1)S(1)} collective-permute-done((bf16[160,512]{1,0:T(8,128)(2,1)S(1)}, bf16[160,512]{1,0:T(8,128)(2,1)S(1)}, u32[]{:S(2)}, u32[]{:S(2)}) %collective-permute-start.11) | collective-permute-done | bytes 163872 | tf_op jit(solution)/shard_map/exchange_context/ppermute | solution.py:20
  137.6 0.7 copy-done.17
  138.4 0.9 copy-done.8
  139.3 0.6 collective-permute-start.10
  139.9 0.7 copy-done.19
  140.6 1.2 collective-permute-start.12
  141.8 4.9 %collective-permute-done.10.refs_5_ = bf16[160,512]{1,0:T(8,128)(2,1)} collective-permute-done((bf16[160,512]{1,0:T(8,128)(2,1)}, bf16[160,512]{1,0:T(8,128)(2,1)}, u32[]{:S(2)}, u32[]{:S(2)}) %collective-permute-start.10) | collective-permute-done | bytes 163872 | tf_op jit(solution)/shard_map/exchange_context/ppermute | solution.py:20
  146.7 2.4 %collective-permute-done.12.refs_7_ = bf16[160,512]{1,0:T(8,128)(2,1)} collective-permute-done((bf16[160,512]{1,0:T(8,128)(2,1)}, bf16[160,512]{1,0:T(8,128)(2,1)}, u32[]{:S(2)}, u32[]{:S(2)}) %collective-permute-start.12) | collective-permute-done | bytes 163872 | tf_op jit(solution)/shard_map/exchange_context/ppermute | solution.py:20
  149.1 1.1 copy-done.3
  150.3 1.1 copy-done.5
  151.4 1.1 copy-done.7
  152.6 1.1 copy-done.9
  153.7 0.9 copy-done.14
  154.6 0.9 copy-done.16
  155.5 0.9 copy-done.18
  156.5 0.9 copy-done.20
  157.4 11.6 %mixer.3 = (bf16[256,1280]{1,0:T(8,128)(2,1)}, f32[256,1280]{1,0:T(8,128)}) custom-call(s32[4]{0:T(128)S(1)} %pad_add_fusion.1.place, bf16[160,512]{1,0:T(8,128)(2,1)S(1)} %get-tuple-element.32.refs_0_, bf16[160,512]{1,0:T(8,128)(2,1)} %get-tuple-element.34.refs_1_, bf16[160,512]{1,0:T(8,128)(2,1)S(1)} %copy-done.14, bf16[160,512]{1,0:T(8,128)(2,1)S(1)} %copy-done.20, ...), custom_call_target="tpu_custom_call" | custom-call | flops 5000000000 | bytes 20000000 | tf_op jit(solution)/shard_map/mixer/mixer/pallas_call | solution.py:265
  169.0 0.9 collective-permute-start.19
  169.9 11.8 %mixer.2 = (bf16[256,1280]{1,0:T(8,128)(2,1)}, f32[256,1280]{1,0:T(8,128)}) custom-call(s32[4]{0:T(128)S(1)} %pad_add_fusion.1.place, bf16[160,512]{1,0:T(8,128)(2,1)S(1)} %get-tuple-element.32.refs_0_, bf16[160,512]{1,0:T(8,128)(2,1)} %get-tuple-element.34.refs_1_, bf16[160,512]{1,0:T(8,128)(2,1)S(1)} %copy-done.14, bf16[160,512]{1,0:T(8,128)(2,1)S(1)} %copy-done.20, ...), custom_call_target="tpu_custom_call" | custom-call | flops 5000000000 | bytes 20000000 | tf_op jit(solution)/shard_map/mixer/mixer/pallas_call | solution.py:265
  181.7 1.3 collective-permute-start.18
  183.0 0.6 reduce-window.6
  183.9 3.1 %collective-permute-done.19.received = bf16[256,1280]{1,0:T(8,128)(2,1)} collective-permute-done((bf16[256,1280]{1,0:T(8,128)(2,1)}, bf16[256,1280]{1,0:T(8,128)(2,1)}, u32[]{:S(2)}, u32[]{:S(2)}) %collective-permute-start.19) | collective-permute-done | bytes 655392 | tf_op jit(solution)/shard_map/mixer/ppermute | solution.py:20
  187.0 1.3 copy-done.12
  188.3 2.9 %gather.1.earlier = bf16[4,256,1280]{2,1,0:T(8,128)(2,1)S(1)} custom-call(s32[4]{0:T(128)S(1)} %pad_add_fusion.1.place, s32[4,256]{1,0:T(4,128)S(1)} %subtract_bitcast_fusion.index_ref, f32[256,1280]{1,0:T(8,128)S(1)} %copy-done.12, bf16[256,1280]{1,0:T(8,128)(2,1)} %collective-permute-done.19.received, f32[1,1280]{1,0:T(1,128)S(1)} %reshape.88.gain_ref), custom_call_target="tpu_custom_call" | custom-call | flops 1000000000 | bytes 5000000 | tf_op jit(solution)/shard_map/merge/gather/pallas_call | solution.py:315
  191.2 9.3 %collective-permute-done.18.received = bf16[256,1280]{1,0:T(8,128)(2,1)} collective-permute-done((bf16[256,1280]{1,0:T(8,128)(2,1)}, bf16[256,1280]{1,0:T(8,128)(2,1)}, u32[]{:S(2)}, u32[]{:S(2)}) %collective-permute-start.18) | collective-permute-done | bytes 655392 | tf_op jit(solution)/shard_map/mixer/ppermute | solution.py:20
  200.5 6.7 %merge.1 = (f32[256,320]{1,0:T(8,128)S(1)}, f32[256,320]{1,0:T(8,128)S(1)}) custom-call(s32[4]{0:T(128)S(1)} %pad_add_fusion.1.place, s32[4,256]{1,0:T(4,128)S(1)} %subtract_bitcast_fusion.index_ref, f32[256,1280]{1,0:T(8,128)S(1)} %copy-done.11, bf16[256,1280]{1,0:T(8,128)(2,1)} %collective-permute-done.18.received, f32[1,1280]{1,0:T(1,128)S(1)} %reshape.88.gain_ref, ...), custom_call_target="tpu_custom_call" | custom-call | flops 3000000000 | bytes 12000000 | tf_op jit(solution)/shard_map/merge/merge/pallas_call | solution.py:351
  207.2 0.7 copy-done.21
  208.0 0.6 bitcast_add_fusion.position
  208.6 1.0 collective-permute-done.21.received
  209.6 0.8 copy-done.30
  210.4 2.2 place.1
  212.6 18.1 %all_to_all.5 = bf16[8,64,320]{2,1,0:T(8,128)(2,1)S(1)} all-to-all(bf16[8,64,320]{2,1,0:T(8,128)(2,1)} %bitcast.46), channel_id=1, replica_groups=mesh['req'=8,'tp'=4] {'req'}, dimensions={0} | all-to-all | bytes 655360 | tf_op jit(solution)/shard_map/place/all_to_all | solution.py:502
  230.7 0.7 copy.14
  (97 shorter events, 1.7 us)
Async XLA Ops:
  0.0 19.7 %copy-start.32 = (s32[1024]{0:T(1024)S(1)}, s32[1024]{0:T(1024)}, u32[]{:S(2)}) copy-start(s32[1024]{0:T(1024)} %param.13) | copy-start | bytes 12292
  0.7 1.7 copy-start
  2.4 1.7 copy-start.10
  11.4 0.7 copy-start.24
  12.1 50.1 %collective-permute-start = (bf16[160,1024]{1,0:T(8,128)(2,1)S(1)}, bf16[160,1024]{1,0:T(8,128)(2,1)S(1)}, u32[]{:S(2)}, u32[]{:S(2)}) collective-permute-start(bf16[160,1024]{1,0:T(8,128)(2,1)S(1)} %get-tuple-element.18), channel_id=1, source_target_pairs={{0,4},{4,0},{8,12},{12,8},{16,20},{20,16},{24,28},{28,24},{1,5},{5... | collective-permute-start | bytes 983048 | tf_op jit(solution)/shard_map/exchange_keys/ppermute | solution.py:20
  15.1 53.8 %collective-permute-start.1 = (bf16[320,1024]{1,0:T(8,128)(2,1)}, bf16[320,1024]{1,0:T(8,128)(2,1)S(1)}, u32[]{:S(2)}, u32[]{:S(2)}) collective-permute-start(bf16[320,1024]{1,0:T(8,128)(2,1)} %get-tuple-element.19.refs_2_), channel_id=1, source_target_pairs={{0,8},{4,12},{8,16},{12,20},{16,24},{20,28},{1,9},{5,13},{9,17},{1... | collective-permute-start | bytes 1966088 | tf_op jit(solution)/shard_map/exchange_keys/ppermute | solution.py:26
  18.6 45.6 %collective-permute-start.2 = (bf16[320,1024]{1,0:T(8,128)(2,1)S(1)}, bf16[320,1024]{1,0:T(8,128)(2,1)}, u32[]{:S(2)}, u32[]{:S(2)}) collective-permute-start(bf16[320,1024]{1,0:T(8,128)(2,1)S(1)} %get-tuple-element.20), channel_id=1, source_target_pairs={{0,4},{4,0},{8,12},{12,8},{16,20},{20,16},{24,28},{28,24},{1,5},{5... | collective-permute-start | bytes 1966088 | tf_op jit(solution)/shard_map/exchange_keys/ppermute | solution.py:20
  19.2 130.0 %collective-permute-start.16 = (bf16[1280,1280]{1,0:T(8,128)(2,1)}, bf16[1280,1280]{1,0:T(8,128)(2,1)}, u32[]{:S(2)}, u32[]{:S(2)}) collective-permute-start(bf16[1280,1280]{1,0:T(8,128)(2,1)} %refs_14_.3), channel_id=1, source_target_pairs={{0,1},{1,0},{2,3},{3,2},{4,5},{5,4},{6,7},{7,6},{8,9},{9,8},{10,11... | collective-permute-start | bytes 9830408 | tf_op jit(solution)/shard_map/weights/ppermute | solution.py:20
  19.2 130.0 %collective-permute-start.17 = (bf16[1280,1280]{1,0:T(8,128)(2,1)}, bf16[1280,1280]{1,0:T(8,128)(2,1)}, u32[]{:S(2)}, u32[]{:S(2)}) collective-permute-start(bf16[1280,1280]{1,0:T(8,128)(2,1)} %refs_16_.3), channel_id=1, source_target_pairs={{0,1},{1,0},{2,3},{3,2},{4,5},{5,4},{6,7},{7,6},{8,9},{9,8},{10,11... | collective-permute-start | bytes 9830408 | tf_op jit(solution)/shard_map/weights/ppermute | solution.py:20
  62.2 0.7 copy-start.27
  62.9 33.4 %collective-permute-start.4 = (bf16[320,1024]{1,0:T(8,128)(2,1)}, bf16[320,1024]{1,0:T(8,128)(2,1)S(1)}, u32[]{:S(2)}, u32[]{:S(2)}) collective-permute-start(bf16[320,1024]{1,0:T(8,128)(2,1)} %get-tuple-element.19.refs_2_), channel_id=1, source_target_pairs={{8,0},{12,4},{16,8},{20,12},{24,16},{28,20},{9,1},{13,5},{17,9},{2... | collective-permute-start | bytes 1966088 | tf_op jit(solution)/shard_map/exchange_keys/ppermute | solution.py:26
  64.2 32.2 %collective-permute-start.3 = (bf16[320,1024]{1,0:T(8,128)(2,1)}, bf16[320,1024]{1,0:T(8,128)(2,1)S(1)}, u32[]{:S(2)}, u32[]{:S(2)}) collective-permute-start(bf16[320,1024]{1,0:T(8,128)(2,1)} %collective-permute-done.2.refs_3_), channel_id=1, source_target_pairs={{0,8},{4,12},{8,16},{12,20},{16,24},{20,28},{1,9},{5,13},{9,17},{1... | collective-permute-start | bytes 1966088 | tf_op jit(solution)/shard_map/exchange_keys/ppermute | solution.py:26
  68.8 0.8 copy-start.22
  69.7 28.4 %collective-permute-start.5 = (bf16[320,1024]{1,0:T(8,128)(2,1)}, bf16[320,1024]{1,0:T(8,128)(2,1)S(1)}, u32[]{:S(2)}, u32[]{:S(2)}) collective-permute-start(bf16[320,1024]{1,0:T(8,128)(2,1)} %collective-permute-done.2.refs_3_), channel_id=1, source_target_pairs={{8,0},{12,4},{16,8},{20,12},{24,16},{28,20},{9,1},{13,5},{17,9},{2... | collective-permute-start | bytes 1966088 | tf_op jit(solution)/shard_map/exchange_keys/ppermute | solution.py:26
  71.0 1.0 copy-start.25
  71.9 1.0 copy-start.28
  72.9 23.4 %copy-start.2 = (bf16[320,1280]{1,0:T(8,128)(2,1)S(1)}, bf16[320,1280]{1,0:T(8,128)(2,1)}, u32[]{:S(2)}) copy-start(bf16[320,1280]{1,0:T(8,128)(2,1)} %param.16) | copy-start | bytes 2457604
  72.9 25.1 %copy-start.1 = (bf16[5120,320]{0,1:T(8,128)(2,1)S(1)}, bf16[5120,320]{0,1:T(8,128)(2,1)}, u32[]{:S(2)}) copy-start(bf16[5120,320]{0,1:T(8,128)(2,1)} %param.21) | copy-start | bytes 9830404
  72.9 25.3 %copy-start.23 = (bf16[320,1024]{1,0:T(8,128)(2,1)S(1)}, bf16[320,1024]{1,0:T(8,128)(2,1)}, u32[]{:S(2)}) copy-start(bf16[320,1024]{1,0:T(8,128)(2,1)} %copy-done.22) | copy-start | bytes 1966084
  72.9 25.3 %copy-start.26 = (bf16[160,1024]{1,0:T(8,128)(2,1)S(1)}, bf16[160,1024]{1,0:T(8,128)(2,1)}, u32[]{:S(2)}) copy-start(bf16[160,1024]{1,0:T(8,128)(2,1)} %copy-done.24) | copy-start | bytes 983044
  72.9 25.3 %copy-start.29 = (bf16[160,1024]{1,0:T(8,128)(2,1)S(1)}, bf16[160,1024]{1,0:T(8,128)(2,1)}, u32[]{:S(2)}) copy-start(bf16[160,1024]{1,0:T(8,128)(2,1)} %copy-done.27) | copy-start | bytes 983044
  96.4 6.1 %collective-permute-start.13 = (bf16[2,160,1280]{2,1,0:T(8,128)(2,1)S(1)}, bf16[2,160,1280]{2,1,0:T(8,128)(2,1)S(1)}, u32[]{:S(2)}, u32[]{:S(2)}) collective-permute-start(bf16[2,160,1280]{2,1,0:T(8,128)(2,1)S(1)} %bitcast.40), channel_id=1, source_target_pairs={{0,1},{1,0},{2,3},{3,2},{4,5},{5,4},{6,7},{7,6},{8,9},{9,8},{10,11... | collective-permute-start | bytes 2457608 | tf_op jit(solution)/shard_map/weights/ppermute | solution.py:20
  96.4 20.7 %collective-permute-start.14 = (bf16[2,160,1280]{2,1,0:T(8,128)(2,1)S(1)}, bf16[2,160,1280]{2,1,0:T(8,128)(2,1)S(1)}, u32[]{:S(2)}, u32[]{:S(2)}) collective-permute-start(bf16[2,160,1280]{2,1,0:T(8,128)(2,1)S(1)} %bitcast.41), channel_id=1, source_target_pairs={{0,2},{1,3},{2,0},{3,1},{4,6},{5,7},{6,4},{7,5},{8,10},{9,11},{10,... | collective-permute-start | bytes 2457608 | tf_op jit(solution)/shard_map/weights/ppermute | solution.py:20
  98.0 93.1 %collective-permute-start.20 = (bf16[320,5120]{1,0:T(8,128)(2,1)S(1)}, bf16[320,5120]{1,0:T(8,128)(2,1)}, u32[]{:S(2)}, u32[]{:S(2)}) collective-permute-start(bf16[320,5120]{1,0:T(8,128)(2,1)S(1)} %bitcast.38), channel_id=1, source_target_pairs={{0,1},{1,0},{2,3},{3,2},{4,5},{5,4},{6,7},{7,6},{8,9},{9,8},{10,11... | collective-permute-start | bytes 9830408 | tf_op jit(solution)/shard_map/weights/ppermute | solution.py:20
  98.2 43.5 %copy-start.33 = (bf16[1280]{0:T(1024)(128)(2,1)S(1)}, bf16[1280]{0:T(1024)(128)(2,1)}, u32[]{:S(2)}) copy-start(bf16[1280]{0:T(1024)(128)(2,1)} %param.17) | copy-start | bytes 7684
  102.5 0.9 copy-start.4
  103.4 15.2 %collective-permute-start.7 = (bf16[160,512]{1,0:T(8,128)(2,1)S(1)}, bf16[160,512]{1,0:T(8,128)(2,1)S(1)}, u32[]{:S(2)}, u32[]{:S(2)}) collective-permute-start(bf16[160,512]{1,0:T(8,128)(2,1)S(1)} %get-tuple-element.31), channel_id=1, source_target_pairs={{0,1},{1,0},{2,3},{3,2},{4,5},{5,4},{6,7},{7,6},{8,9},{9,8},{10,11... | collective-permute-start | bytes 491528 | tf_op jit(solution)/shard_map/exchange_context/ppermute | solution.py:20
  117.1 5.8 %collective-permute-start.9 = (bf16[160,512]{1,0:T(8,128)(2,1)S(1)}, bf16[160,512]{1,0:T(8,128)(2,1)S(1)}, u32[]{:S(2)}, u32[]{:S(2)}) collective-permute-start(bf16[160,512]{1,0:T(8,128)(2,1)S(1)} %get-tuple-element.32.refs_0_), channel_id=1, source_target_pairs={{0,2},{1,3},{2,0},{3,1},{4,6},{5,7},{6,4},{7,5},{8,10},{9,11},{10,... | collective-permute-start | bytes 491528 | tf_op jit(solution)/shard_map/exchange_context/ppermute | solution.py:20
  118.6 0.7 copy-start.13
  119.3 19.1 %collective-permute-start.15 = (bf16[2,160,1280]{2,1,0:T(8,128)(2,1)S(1)}, bf16[2,160,1280]{2,1,0:T(8,128)(2,1)S(1)}, u32[]{:S(2)}, u32[]{:S(2)}) collective-permute-start(bf16[2,160,1280]{2,1,0:T(8,128)(2,1)S(1)} %collective-permute-done.14.refs_12_), channel_id=1, source_target_pairs={{0,1},{1,0},{2,3},{3,2},{4,5},{5,4},{6,7},{7,6},{8,9},{9,8},{10,11... | collective-permute-start | bytes 2457608 | tf_op jit(solution)/shard_map/weights/ppermute | solution.py:20
  119.3 0.9 copy-start.6
  122.8 15.6 %copy-start.15 = (bf16[160,512]{1,0:T(8,128)(2,1)}, bf16[160,512]{1,0:T(8,128)(2,1)S(1)}, u32[]{:S(2)}) copy-start(bf16[160,512]{1,0:T(8,128)(2,1)S(1)} %collective-permute-done.9.refs_4_) | copy-start | bytes 491524
  122.9 8.4 %collective-permute-start.6 = (bf16[2,160,512]{2,1,0:T(8,128)(2,1)S(1)}, bf16[2,160,512]{2,1,0:T(8,128)(2,1)S(1)}, u32[]{:S(2)}, u32[]{:S(2)}) collective-permute-start(bf16[2,160,512]{2,1,0:T(8,128)(2,1)S(1)} %slice.68), channel_id=1, source_target_pairs={{0,4},{4,0},{8,12},{12,8},{16,20},{20,16},{24,28},{28,24},{1,5},{5... | collective-permute-start | bytes 983048 | tf_op jit(solution)/shard_map/exchange_context/ppermute | solution.py:20
  131.2 6.4 %collective-permute-start.11 = (bf16[160,512]{1,0:T(8,128)(2,1)S(1)}, bf16[160,512]{1,0:T(8,128)(2,1)S(1)}, u32[]{:S(2)}, u32[]{:S(2)}) collective-permute-start(bf16[160,512]{1,0:T(8,128)(2,1)S(1)} %get-tuple-element.31), channel_id=1, source_target_pairs={{0,3},{1,2},{2,1},{3,0},{4,7},{5,6},{6,5},{7,4},{8,11},{9,10},{10,... | collective-permute-start | bytes 491528 | tf_op jit(solution)/shard_map/exchange_context/ppermute | solution.py:20
  137.6 0.7 copy-start.17
  138.3 1.6 collective-permute-start.8
  138.4 0.9 copy-start.8
  139.3 7.4 %collective-permute-start.10 = (bf16[160,512]{1,0:T(8,128)(2,1)}, bf16[160,512]{1,0:T(8,128)(2,1)}, u32[]{:S(2)}, u32[]{:S(2)}) collective-permute-start(bf16[160,512]{1,0:T(8,128)(2,1)} %get-tuple-element.34.refs_1_), channel_id=1, source_target_pairs={{0,2},{1,3},{2,0},{3,1},{4,6},{5,7},{6,4},{7,5},{8,10},{9,11},{10,... | collective-permute-start | bytes 491528 | tf_op jit(solution)/shard_map/exchange_context/ppermute | solution.py:20
  139.9 0.7 copy-start.19
  140.6 8.5 %collective-permute-start.12 = (bf16[160,512]{1,0:T(8,128)(2,1)}, bf16[160,512]{1,0:T(8,128)(2,1)}, u32[]{:S(2)}, u32[]{:S(2)}) collective-permute-start(bf16[160,512]{1,0:T(8,128)(2,1)} %get-tuple-element.33), channel_id=1, source_target_pairs={{0,3},{1,2},{2,1},{3,0},{4,7},{5,6},{6,5},{7,4},{8,11},{9,10},{10,... | collective-permute-start | bytes 491528 | tf_op jit(solution)/shard_map/exchange_context/ppermute | solution.py:20
  149.1 1.1 copy-start.3
  150.3 1.1 copy-start.5
  151.4 1.1 copy-start.7
  152.6 1.1 copy-start.9
  153.7 0.9 copy-start.14
  154.6 0.9 copy-start.16
  155.5 0.9 copy-start.18
  156.5 0.9 copy-start.20
  169.0 14.0 %copy-start.31 = (s32[256,1]{0,1:T(1,128)S(1)}, s32[256,1]{0,1:T(1,128)}, u32[]{:S(2)}) copy-start(s32[256,1]{0,1:T(1,128)} %param.23) | copy-start | bytes 3076
  169.0 14.8 %copy-start.34 = (bf16[1280]{0:T(1024)(128)(2,1)S(1)}, bf16[1280]{0:T(1024)(128)(2,1)}, u32[]{:S(2)}) copy-start(bf16[1280]{0:T(1024)(128)(2,1)} %param.20) | copy-start | bytes 7684
  169.0 14.8 %copy-start.35 = (s32[256,4]{0,1:T(4,128)S(1)}, s32[256,4]{0,1:T(4,128)}, u32[]{:S(2)}) copy-start(s32[256,4]{0,1:T(4,128)} %param.22) | copy-start | bytes 12292
  169.0 17.9 %collective-permute-start.19 = (bf16[256,1280]{1,0:T(8,128)(2,1)}, bf16[256,1280]{1,0:T(8,128)(2,1)}, u32[]{:S(2)}, u32[]{:S(2)}) collective-permute-start(bf16[256,1280]{1,0:T(8,128)(2,1)} %get-tuple-element.26), channel_id=1, source_target_pairs={{0,2},{1,3},{2,0},{3,1},{4,6},{5,7},{6,4},{7,5},{8,10},{9,11},{10,... | collective-permute-start | bytes 1966088 | tf_op jit(solution)/shard_map/mixer/ppermute | solution.py:20
  181.7 18.7 %collective-permute-start.18 = (bf16[256,1280]{1,0:T(8,128)(2,1)}, bf16[256,1280]{1,0:T(8,128)(2,1)}, u32[]{:S(2)}, u32[]{:S(2)}) collective-permute-start(bf16[256,1280]{1,0:T(8,128)(2,1)} %get-tuple-element.24), channel_id=1, source_target_pairs={{0,2},{1,3},{2,0},{3,1},{4,6},{5,7},{6,4},{7,5},{8,10},{9,11},{10,... | collective-permute-start | bytes 1966088 | tf_op jit(solution)/shard_map/mixer/ppermute | solution.py:20
  183.8 16.6 %copy-start.11 = (f32[256,1280]{1,0:T(8,128)S(1)}, f32[256,1280]{1,0:T(8,128)}, u32[]{:S(2)}) copy-start(f32[256,1280]{1,0:T(8,128)} %get-tuple-element.23.kept) | copy-start | bytes 3932164
  187.0 1.3 copy-start.12
  207.2 0.7 copy-start.21
  207.9 1.7 collective-permute-start.21
  209.6 0.8 copy-start.30
where the time goes:
time: 231 us
  Pallas kernels  70 us (30%)
  blocking collectives  59.5 us (26%)
  waiting for transfers between devices  49.2 us (21%)
  local copies, waits for them, and re-layouts  26.8 us (12%)
  starting transfers between devices  24 us (10%)
    ppermute x18, waiting for transfers between devices, swap(): lax.ppermute(block, axis, [(i, i ^ flip) for i in range(lax.axis_size(axi...  49.2 us
    all_gather x1, blocking collectives, body(): every = lax.all_gather(segments, 'req', axis=0, tiled=True)  41.4 us
    pallas_call x2, Pallas kernels, attend(): pl.pallas_call(functools.partial(attend_kernel, blocks, base, state is No...  27.6 us
    unnamed x73, local copies, waits for them, and re-layouts  24.2 us
    pallas_call x2, Pallas kernels, mixer(): pl.pallas_call(mixer_kernel, grid_spec=pltpu.PrefetchScalarGridSpec(num_s...  23.4 us
    all_to_all x1, blocking collectives, body(): lax.all_to_all(outgoing, 'req', split_axis=0, concat_axis=0, tiled=True)  18.1 us
    ppermute x18, starting transfers between devices, swap(): lax.ppermute(block, axis, [(i, i ^ flip) for i in range(lax.axis_size(axi...  13.3 us
    ppermute x4, starting transfers between devices, shifted(): return lax.ppermute(block, axis, route)  10.7 us
  transfers between devices with their start and end apart: 22, of which 9 were waited for; matrix products, arithmetic and copies ran while one was open for 1% of the time, Pallas kernels for 23%

commit v1 on v0

--- a/solution.py
+++ b/solution.py
@@ -13,7 +13,8 @@
 MASKED = -1e30
 START = -1e28
 FACTOR = 1.0 / math.sqrt(HD)
-MIB = 1 << 20
+SEGMENT_ROWS = 16
+VROWS = 96
 
 
 def swap(block, axis, flip):
@@ -41,26 +42,32 @@
 NT = ((1,), (1,))
 
 
-def vmem(limit):
-    return pltpu.CompilerParams(vmem_limit_bytes=limit * MIB)
-
-
-def project_kernel(par_ref, x_ref, gain_ref, w_ref, kv_keep, kv_send, q_keep, q_send):
+def vmem():
+    return pltpu.CompilerParams(vmem_limit_bytes=60 << 20)
+
+
+def project_kernel(par_ref, x_ref, segment_ref, gain_ref, w_ref, kv_keep, kv_send, q_keep, q_send):
     par = par_ref[0]
     half = w_ref.shape[2]
     rows = normalized(x_ref[...].astype(jnp.float32), gain_ref[...])
+    number = segment_ref[...] + 1
+    row = lax.broadcasted_iota(jnp.int32, (SEGMENT_ROWS, 1), 0)
+    number = jnp.where(row == 0, number & 255, jnp.where(row == 1, number >> 8, 0))
+    number = number.astype(jnp.float32).astype(jnp.bfloat16)
     for which, kv, q in ((par, kv_keep, q_keep), (1 - par, kv_send, q_send)):
         for part in (1, 2):
             out = dot(w_ref[part, which], rows, NT).astype(jnp.bfloat16)
             kv[(part - 1) * half : part * half, :] = out
+        kv[2 * half :, :] = number
         q[...] = dot(w_ref[0, which], rows, NT).astype(jnp.bfloat16)
 
 
-def project(par, tokens, gain, weight):
+def project(par, tokens, segments, gain, weight):
     rows, width = tokens.shape
     half = weight.shape[2]
     step = 256
-    shapes = [(2 * half, rows), (2 * half, rows), (half, rows), (half, rows)]
+    tall = 2 * half + SEGMENT_ROWS
+    shapes = [(tall, rows), (tall, rows), (half, rows), (half, rows)]
     return pl.pallas_call(
         project_kernel,
         grid_spec=pltpu.PrefetchScalarGridSpec(
@@ -68,80 +75,93 @@
             grid=(rows // step,),
             in_specs=[
                 pl.BlockSpec((step, width), lambda i, s: (i, 0)),
+                pl.BlockSpec((1, step), lambda i, s: (0, i)),
                 pl.BlockSpec((1, width), lambda i, s: (0, 0)),
                 pl.BlockSpec(weight.shape, lambda i, s: (0, 0, 0, 0)),
             ],
             out_specs=[pl.BlockSpec((s[0], step), lambda i, s: (0, i)) for s in shapes],
         ),
         out_shape=[jax.ShapeDtypeStruct(s, jnp.bfloat16) for s in shapes],
-        compiler_params=vmem(32),
+        compiler_params=vmem(),
         name="project",
-    )(par, tokens, gain, weight)
-
-
-def attend_kernel(blocks, base, first, last, meta, *refs):
-    q_refs, refs = refs[:2], refs[2:]
+    )(par, tokens, segments, gain, weight)
+
+
+def numbers_of(ref, at):
+    two = ref[:, at].astype(jnp.float32)
+    return two[0:1] + 256.0 * two[1:2]
+
+
+def attend_kernel(blocks, fresh, skip, last, place, *refs):
+    q_refs, number_refs, refs = refs[:2], refs[2:4], refs[4:]
     kv_refs, refs = refs[:blocks], refs[blocks:]
-    q_segment, k_segment, refs = refs[0], refs[1], refs[2:]
-    if first:
-        acc_out, ml_out, refs = refs[0], refs[1], refs[2:]
+    if fresh:
+        acc_in, peak_in, refs = refs[0], refs[1], refs[2:]
+    if last:
+        ctx_out, refs = refs[0], refs[1:]
     else:
-        acc_in, ml_in, ctx_out, refs = refs[0], refs[1], refs[2], refs[3:]
-    keys, values, columns, acc, ml = refs
-    heads = 2
+        acc_out, peak_out, refs = refs[0], refs[1], refs[2:]
+    keys, values, columns, acc, peak, bounds = refs
     tiles_of = kv_refs[0].shape[1] // TILE
     tiles = blocks * tiles_of
+    tall = kv_refs[0].shape[0] - SEGMENT_ROWS
     j = pl.program_id(0)
 
     @pl.when(j == 0)
     def _():
         for b in range(blocks):
             for t in range(tiles_of):
+                n = b * tiles_of + t
                 at = slice(t * TILE, (t + 1) * TILE)
-                for h in range(heads):
+                for h in range(2):
                     block = kv_refs[b][h * HD : (h + 1) * HD, at].astype(jnp.float32)
-                    keys[b * tiles_of + t, h] = jnp.transpose(block).astype(jnp.bfloat16)
-                    values[b * tiles_of + t, h] = kv_refs[b][
-                        (heads + h) * HD : (heads + h + 1) * HD, at
-                    ]
-                row = jnp.broadcast_to(k_segment[b : b + 1, at], (128, TILE))
-                columns[b * tiles_of + t] = jnp.transpose(row)
-
-    if first:
+                    keys[n, h] = jnp.transpose(block).astype(jnp.bfloat16)
+                    values[n, h, :HD] = kv_refs[b][(2 + h) * HD : (3 + h) * HD, at]
+                    values[n, h, HD:] = jnp.ones((VROWS - HD, TILE), jnp.bfloat16)
+                number = numbers_of(kv_refs[b].at[tall:], at)
+                bounds[2 * n] = jnp.min(number)
+                bounds[2 * n + 1] = jnp.max(number)
+                columns[n] = jnp.transpose(jnp.broadcast_to(number, (128, TILE)))
+
+    def start():
         acc[...] = jnp.zeros_like(acc)
-        ml[0:2, :] = jnp.full((2, TILE), START, jnp.float32)
-        ml[2:4, :] = jnp.zeros((2, TILE), jnp.float32)
+        peak[...] = jnp.full_like(peak, START)
+
+    def go_on():
+        acc[...] = acc_in[0]
+        peak[...] = peak_in[0]
+
+    if fresh:
+        pl.when(j < fresh)(go_on)
+        pl.when(j >= fresh)(start)
     else:
-        acc[...] = acc_in[0]
-        ml[...] = ml_in[0]
+        start()
 
     queries = jnp.where(j < 2, q_refs[0][...], q_refs[1][...])
-    q_low, q_high = meta[2 + 2 * j], meta[3 + 2 * j]
-    q_row = q_segment[0]
+    whole_tile = slice(0, TILE)
+    q_row = jnp.where(
+        j < 2, numbers_of(number_refs[0], whole_tile), numbers_of(number_refs[1], whole_tile)
+    )
+    q_low, q_high = jnp.min(q_row), jnp.max(q_row)
 
     def update(t, masked):
         if masked:
             column = columns[t]
             matches = jnp.concatenate([column] * (TILE // 128), axis=1) == q_row
-        for h in range(heads):
-            scores = dot(keys[t, h], queries[h * HD : (h + 1) * HD, :], NN)
+        scores = [dot(keys[t, h], queries[h * HD : (h + 1) * HD, :], NN) for h in range(2)]
+        for h in range(2):
+            here = scores[h]
             if masked:
-                scores = jnp.where(matches, scores, MASKED)
-            old = ml[h : h + 1, :]
-            new = jnp.maximum(old, jnp.max(scores, axis=0, keepdims=True))
-            probs = jnp.exp((scores - new) * FACTOR)
+                here = jnp.where(matches, here, MASKED)
+            old = peak[h : h + 1, :]
+            new = jnp.maximum(old, jnp.max(here, axis=0, keepdims=True))
+            probs = jnp.exp((here - new) * FACTOR)
             shrink = jnp.exp((old - new) * FACTOR)
-            ml[h : h + 1, :] = new
-            ml[2 + h : 3 + h, :] = ml[2 + h : 3 + h, :] * shrink + jnp.sum(
-                probs, axis=0, keepdims=True
-            )
-            acc[h * HD : (h + 1) * HD, :] = acc[h * HD : (h + 1) * HD, :] * shrink + dot(
-                values[t, h], probs.astype(jnp.bfloat16), NN
-            )
+            peak[h : h + 1, :] = new
+            acc[h] = acc[h] * shrink + dot(values[t, h], probs.astype(jnp.bfloat16), NN)
 
     def visit(t, carry):
-        at = 10 + 2 * (base * tiles_of + t)
-        k_low, k_high = meta[at], meta[at + 1]
+        k_low, k_high = bounds[2 * t], bounds[2 * t + 1]
         touches = (k_high >= q_low) & (k_low <= q_high)
         whole = (k_low == k_high) & (q_low == q_high)
 
@@ -155,60 +175,72 @@
 
         return carry
 
-    lax.fori_loop(0, tiles, visit, 0)
-    if first:
+    lax.fori_loop(jnp.where(j < fresh, skip, 0), tiles, visit, 0)
+    if last:
+        for h in range(2):
+            at = slice(h * HD, (h + 1) * HD)
+            ctx_out[0, at, :] = (acc[h, :HD] / acc[h, HD : HD + 1]).astype(jnp.bfloat16)
+    else:
         acc_out[0] = acc[...]
-        ml_out[0] = ml[...]
-    else:
-        for h in range(heads):
-            at = slice(h * HD, (h + 1) * HD)
-            ctx_out[0, at, :] = (acc[at, :] / ml[2 + h : 3 + h, :]).astype(jnp.bfloat16)
-
-
-def attend(meta, q_own, q_peer, key_values, q_segment, k_segment, base, state=None):
-    half, rows = q_own.shape
+        peak_out[0] = peak[...]
+
+
+def attend(place, queries, numbers, key_values, name, state=None, skip=0, last=False):
+    half, rows = queries[0].shape
+    steps = 2 * len(queries)
     blocks = len(key_values)
     tiles = blocks * rows // TILE
+    tall = key_values[0].shape[0] - SEGMENT_ROWS
+    fresh = 0 if state is None else state[0].shape[0]
+    queries = [queries[0], queries[-1]]
+    numbers = [numbers[0], numbers[-1]]
     q_spec = pl.BlockSpec((half, TILE), lambda j, s: (0, (j % 2) ^ s[1]))
+    n_spec = pl.BlockSpec((SEGMENT_ROWS, TILE), lambda j, s: (tall // SEGMENT_ROWS, (j % 2) ^ s[1]))
     whole = lambda a: pl.BlockSpec(a.shape, lambda j, s: (0,) * a.ndim)
-    acc_spec = pl.BlockSpec((1, half, TILE), lambda j, s: (j, 0, 0))
-    ml_spec = pl.BlockSpec((1, 4, TILE), lambda j, s: (j, 0, 0))
-    in_specs = [q_spec, q_spec] + [whole(kv) for kv in key_values]
-    in_specs += [pl.BlockSpec((1, 1, TILE), lambda j, s: (j, 0, 0)), whole(k_segment)]
-    operands = [q_own, q_peer, *key_values, q_segment, k_segment]
-    if state is None:
-        out_specs = [acc_spec, ml_spec]
+    acc_shape, peak_shape = (2, VROWS, TILE), (2, TILE)
+    in_specs = [q_spec, q_spec, n_spec, n_spec] + [whole(kv) for kv in key_values]
+    operands = [*queries, *numbers, *key_values]
+    if state is not None:
+        in_specs += [
+            pl.BlockSpec((1,) + acc_shape, lambda j, s: (jnp.minimum(j, fresh - 1), 0, 0, 0)),
+            pl.BlockSpec((1,) + peak_shape, lambda j, s: (jnp.minimum(j, fresh - 1), 0, 0)),
+        ]
+        operands += list(state)
+    if last:
+        out_specs = pl.BlockSpec((1, half, TILE), lambda j, s: (j, 0, 0))
+        out_shape = jax.ShapeDtypeStruct((steps, half, TILE), jnp.bfloat16)
+    else:
+        out_specs = [
+            pl.BlockSpec((1,) + acc_shape, lambda j, s: (j, 0, 0, 0)),
+            pl.BlockSpec((1,) + peak_shape, lambda j, s: (j, 0, 0)),
+        ]
         out_shape = [
-            jax.ShapeDtypeStruct((4, half, TILE), jnp.float32),
-            jax.ShapeDtypeStruct((4, 4, TILE), jnp.float32),
+            jax.ShapeDtypeStruct((steps,) + acc_shape, jnp.float32),
+            jax.ShapeDtypeStruct((steps,) + peak_shape, jnp.float32),
         ]
-    else:
-        in_specs += [acc_spec, ml_spec]
-        operands += list(state)
-        out_specs = acc_spec
-        out_shape = jax.ShapeDtypeStruct((4, half, TILE), jnp.bfloat16)
     return pl.pallas_call(
-        functools.partial(attend_kernel, blocks, base, state is None, state is not None),
+        functools.partial(attend_kernel, blocks, fresh, skip, last),
         grid_spec=pltpu.PrefetchScalarGridSpec(
             num_scalar_prefetch=1,
-            grid=(4,),
+            grid=(steps,),
             in_specs=in_specs,
             out_specs=out_specs,
             scratch_shapes=[
                 pltpu.VMEM((tiles, 2, TILE, HD), jnp.bfloat16),
-                pltpu.VMEM((tiles, 2, HD, TILE), jnp.bfloat16),
+                pltpu.VMEM((tiles, 2, VROWS, TILE), jnp.bfloat16),
                 pltpu.VMEM((tiles, TILE, 128), jnp.float32),
-                pltpu.VMEM((half, TILE), jnp.float32),
-                pltpu.VMEM((4, TILE), jnp.float32),
+                pltpu.VMEM(acc_shape, jnp.float32),
+                pltpu.VMEM(peak_shape, jnp.float32),
+                pltpu.SMEM((2 * tiles,), jnp.float32),
             ],
         ),
         out_shape=out_shape,
-        compiler_params=vmem(40),
+        compiler_params=vmem(),
         cost_estimate=pl.CostEstimate(
-            flops=8_000_000_000, bytes_accessed=8_000_000, transcendentals=8_000_000
-        ),
-        name="attend_local" if state is None else "attend_far",
-    )(meta, *operands)
+            flops=1_000_000_000 * steps * blocks // 2, bytes_accessed=4_000_000, transcendentals=0
+        ),
+        name=name,
+    )(place, *operands)
 
 
 def mixer_kernel(place, *refs):
@@ -286,7 +318,7 @@
             jax.ShapeDtypeStruct((chunk_rows, width), jnp.bfloat16),
             jax.ShapeDtypeStruct((chunk_rows, width), jnp.float32),
         ],
-        compiler_params=vmem(48),
+        compiler_params=vmem(),
         cost_estimate=pl.CostEstimate(
             flops=5_000_000_000, bytes_accessed=20_000_000, transcendentals=0
         ),
@@ -321,7 +353,7 @@
             out_specs=pl.BlockSpec((4, merged_rows, width), lambda i, s: (0, 0, 0)),
         ),
         out_shape=jax.ShapeDtypeStruct((4, merged_rows, width), jnp.bfloat16),
-        compiler_params=vmem(32),
+        compiler_params=vmem(),
         cost_estimate=pl.CostEstimate(
             flops=1_000_000_000, bytes_accessed=5_000_000, transcendentals=0
         ),
@@ -357,7 +389,7 @@
             out_specs=[out_spec, out_spec],
         ),
         out_shape=[jax.ShapeDtypeStruct((merged_rows, columns), jnp.float32)] * 2,
-        compiler_params=vmem(40),
+        compiler_params=vmem(),
         cost_estimate=pl.CostEstimate(
             flops=3_000_000_000, bytes_accessed=12_000_000, transcendentals=0
         ),
@@ -394,39 +426,21 @@
     par = req % 2
     core = lax.axis_index("tp") % 2
 
+    place = jnp.stack([par, core])
     with jax.named_scope("project"):
         weight = jnp.transpose(attend_weight, (1, 2, 0)).reshape(3, 2, half, width)
         kv_own, kv_send, q_own, q_send = project(
-            par.reshape(1), tokens, attend_gain.astype(jnp.float32)[None, :], weight
+            place, tokens, segments[None, :], attend_gain.astype(jnp.float32)[None, :], weight
         )
 
     with jax.named_scope("exchange_keys"):
         kv_peer = swap(kv_send, "req", 1)
         kv_before = shifted(kv_own, "req", 2)
         kv_after = shifted(kv_own, "req", -2)
-        q_peer = swap(q_send, "req", 1)
+        q_send, kv_peer = lax.optimization_barrier((q_send, kv_peer))
         kv_before_peer = shifted(kv_peer, "req", 2)
         kv_after_peer = shifted(kv_peer, "req", -2)
-
-    with jax.named_scope("segments"):
-        every = lax.all_gather(segments, "req", axis=0, tiled=True)
-        every = jnp.pad(every, (2 * rows, 2 * rows), constant_values=-1)
-        window = lax.dynamic_slice_in_dim(every, (req - par) * rows, 6 * rows, 0)
-        window = window.reshape(3, 2, rows)
-        window = jnp.where(par == 0, window, window[:, ::-1])
-        key_rows = jnp.concatenate([window[1], window[0], window[2]], axis=0)
-        tiles = window[1].reshape(2, rows // TILE, TILE)
-        tiles = jnp.where(core == 0, tiles, tiles[:, ::-1]).reshape(4, TILE)
-        key_tiles = key_rows.reshape(-1, TILE)
-        meta = jnp.concatenate(
-            [
-                jnp.stack([par, core]),
-                tiles[:, :: TILE - 1].reshape(-1),
-                key_tiles[:, :: TILE - 1].reshape(-1),
-            ]
-        )
-        q_segment = tiles.astype(jnp.float32)[:, None, :]
-        key_rows = key_rows.astype(jnp.float32)
+        q_peer = swap(q_send, "req", 1)
 
     with jax.named_scope("weights"):
         wo = [output_weight.reshape(2, half, width)]
@@ -439,16 +453,25 @@
         merge_other = swap(merge_own, "tp", 1)
 
     with jax.named_scope("attention"):
-        state = attend(meta, q_own, q_peer, [kv_own, kv_peer], q_segment, key_rows[:2], 0)
+        numbers = [kv_own, kv_peer]
+        state = attend(place, [q_own], [kv_own], [kv_own], "attend_own")
+        state = attend(
+            place,
+            [q_own, q_peer],
+            numbers,
+            [kv_own, kv_peer, kv_before, kv_after],
+            "attend_near",
+            state,
+            skip=rows // TILE,
+        )
         context = attend(
-            meta,
-            q_own,
-            q_peer,
-            [kv_before, kv_before_peer, kv_after, kv_after_peer],
-            q_segment,
-            key_rows[2:],
-            2,
+            place,
+            [q_own, q_peer],
+            numbers,
+            [kv_before_peer, kv_after_peer],
+            "attend_far",
             state,
+            last=True,
         )
 
     with jax.named_scope("exchange_context"):

time: 231 us -> 192 us (0.83); the launches traced: 231 us -> 190 us
  blocking collectives: 59.5 us -> 21 us
  local copies, waits for them, and re-layouts: 26.8 us -> 9.53 us
  Pallas kernels: 70 us -> 84.3 us
  waiting for transfers between devices: 49.2 us -> 46.3 us
    all_gather x1 -> x0, blocking collectives: 41.4 us -> none  [body(): every = lax.all_gather(segments, 'req', axis=0, tiled=True)]
    unnamed x73 -> x23, local copies, waits for them, and re-layouts: 24.2 us -> 3.95 us
    ppermute x18, waiting for transfers between devices: 49.2 us -> 44 us  [swap(): lax.ppermute(block, axis, [(i, i ^ flip) for i in range(lax.axis_size(axi...]
    pallas_call x2 -> x3, Pallas kernels: 27.6 us -> 32.3 us  [attend(): pl.pallas_call(functools.partial(attend_kernel, blocks, fresh, skip, last...]
    pallas_call x1, Pallas kernels: 7.24 us -> 10.5 us  [project(): pl.pallas_call(project_kernel, grid_spec=pltpu.PrefetchScalarGridSpec(num...]
    pallas_call x1, Pallas kernels: 6.66 us -> 9.66 us  [merge(): pl.pallas_call(merge_kernel, grid_spec=pltpu.PrefetchScalarGridSpec(num_s...]
    all_to_all x1, blocking collectives: 18.1 us -> 21 us  [body(): lax.all_to_all(outgoing, 'req', split_axis=0, concat_axis=0, tiled=True)]
    ppermute x4, waiting for transfers between devices: 0.01 us -> 2.35 us  [shifted(): return lax.ppermute(block, axis, route)]
  transfers between devices with their start and end apart: 22 -> 22, of which waited for: 9 -> 11; matrix products, arithmetic and copies ran while one was open for 1% -> 4% of each run, Pallas kernels for 23% -> 33%
where the time goes in v1:
time: 192 us; the launch traced here: 190 us
  Pallas kernels  84.3 us (44%)
  waiting for transfers between devices  46.3 us (24%)
  starting transfers between devices  25.2 us (13%)
  blocking collectives  21 us (11%)
  local copies, waits for them, and re-layouts  9.53 us (5%)
  other arithmetic  3.31 us (2%)
    ppermute x18, waiting for transfers between devices, swap(): lax.ppermute(block, axis, [(i, i ^ flip) for i in range(lax.axis_size(axi...  44 us
    pallas_call x3, Pallas kernels, attend(): pl.pallas_call(functools.partial(attend_kernel, blocks, fresh, skip, last...  32.3 us
    pallas_call x2, Pallas kernels, mixer(): pl.pallas_call(mixer_kernel, grid_spec=pltpu.PrefetchScalarGridSpec(num_s...  24.9 us
    all_to_all x1, blocking collectives, body(): lax.all_to_all(outgoing, 'req', split_axis=0, concat_axis=0, tiled=True)  21 us
    ppermute x18, starting transfers between devices, swap(): lax.ppermute(block, axis, [(i, i ^ flip) for i in range(lax.axis_size(axi...  13.7 us
    ppermute x4, starting transfers between devices, shifted(): return lax.ppermute(block, axis, route)  11.5 us
    pallas_call x1, Pallas kernels, project(): pl.pallas_call(project_kernel, grid_spec=pltpu.PrefetchScalarGridSpec(num...  10.5 us
    pallas_call x1, Pallas kernels, merge(): pl.pallas_call(merge_kernel, grid_spec=pltpu.PrefetchScalarGridSpec(num_s...  9.66 us
  transfers between devices with their start and end apart: 22, of which 11 were waited for; matrix products, arithmetic and copies ran while one was open for 4% of the time, Pallas kernels for 33%

profile of v1, /device:TPU:0, one launch (start us, length us, event | category | flops | bytes accessed | tf_op | source)
XLA Modules:
  0.0 189.9 jit_solution(1573509546163572912)
XLA Ops:
  0.0 1.4 reshape.54.gain_ref
  1.4 0.6 pad_add_fusion.1.par_ref.place
  2.0 10.5 %project.1 = (bf16[336,1024]{1,0:T(8,128)(2,1)}, bf16[336,1024]{1,0:T(8,128)(2,1)}, bf16[160,1024]{1,0:T(8,128)(2,1)}, bf16[160,1024]{1,0:T(8,128)(2,1)}) custom-call(s32[2]{0:T(128)} %pad_add_fusion.1.par_ref.place, bf16[1024,1280]{1,0:T(8,128)(2,1)} %refs_8_.3, s32[1,1024]{1,0:T(1,128)} %bitcast.45, f32[1,1280]{1,0:T(1,128)} %reshape.54.gain_ref, ...), custom_call_target="tpu_custom_call" | custom-call | tf_op jit(solution)/shard_map/project/project/pallas_call | solution.py:71
  12.5 3.0 %collective-permute-start = (bf16[336,1024]{1,0:T(8,128)(2,1)}, bf16[336,1024]{1,0:T(8,128)(2,1)}, u32[]{:S(2)}, u32[]{:S(2)}) collective-permute-start(bf16[336,1024]{1,0:T(8,128)(2,1)} %get-tuple-element.23), channel_id=1, source_target_pairs={{0,4},{4,0},{8,12},{12,8},{16,20},{20,16},{24,28},{28,24},{1,5},{5... | collective-permute-start | bytes 2064392 | tf_op jit(solution)/shard_map/exchange_keys/ppermute | solution.py:21
  15.5 4.3 %collective-permute-start.4 = (bf16[336,1024]{1,0:T(8,128)(2,1)}, bf16[336,1024]{1,0:T(8,128)(2,1)}, u32[]{:S(2)}, u32[]{:S(2)}) collective-permute-start(bf16[336,1024]{1,0:T(8,128)(2,1)} %get-tuple-element.25.refs_2_.refs_3_.refs_4_), channel_id=1, source_target_pairs={{0,8},{4,12},{8,16},{12,20},{16,24},{20,28},{1,9},{5,13},{9,17},{1... | collective-permute-start | bytes 2064392 | tf_op jit(solution)/shard_map/exchange_keys/ppermute | solution.py:27
  19.8 0.5 collective-permute-start.17
  20.3 1.3 collective-permute-start.5
  21.6 9.6 %collective-permute-done.refs_3_.refs_5_ = bf16[336,1024]{1,0:T(8,128)(2,1)} collective-permute-done((bf16[336,1024]{1,0:T(8,128)(2,1)}, bf16[336,1024]{1,0:T(8,128)(2,1)}, u32[]{:S(2)}, u32[]{:S(2)}) %collective-permute-start) | collective-permute-done | bytes 688160 | tf_op jit(solution)/shard_map/exchange_keys/ppermute | solution.py:21
  31.2 4.6 %collective-permute-start.2 = (bf16[336,1024]{1,0:T(8,128)(2,1)}, bf16[336,1024]{1,0:T(8,128)(2,1)}, u32[]{:S(2)}, u32[]{:S(2)}) collective-permute-start(bf16[336,1024]{1,0:T(8,128)(2,1)} %collective-permute-done.refs_3_.refs_5_), channel_id=1, source_target_pairs={{0,8},{4,12},{8,16},{12,20},{16,24},{20,28},{1,9},{5,13},{9,17},{1... | collective-permute-start | bytes 2064392 | tf_op jit(solution)/shard_map/exchange_keys/ppermute | solution.py:27
  35.8 0.0 collective-permute-done.4.refs_6_
  35.8 1.5 collective-permute-start.1
  37.3 7.7 %attend_own.1 = (f32[2,2,96,512]{3,2,1,0:T(8,128)}, f32[2,2,512]{2,1,0:T(2,128)}) custom-call(s32[2]{0:T(128)} %pad_add_fusion.1.par_ref.place, bf16[160,1024]{1,0:T(8,128)(2,1)} %get-tuple-element.21.refs_0_.refs_1_, bf16[160,1024]{1,0:T(8,128)(2,1)} %get-tuple-element.21.refs_0_.refs_1_, bf16[336,1024]{1,0:T(8,128)(2,1)} %get-tuple-element.25.refs_2_.refs_3_.refs_4_, ...), custom_call_target="tpu_custom_call" | custom-call | flops 1000000000 | bytes 4000000 | tf_op jit(solution)/shard_map/attention/attend_own/pallas_call | solution.py:221
  45.0 0.1 collective-permute-start.13
  45.1 1.6 collective-permute-start.14
  46.7 2.3 %collective-permute-done.2.refs_4_ = bf16[336,1024]{1,0:T(8,128)(2,1)} collective-permute-done((bf16[336,1024]{1,0:T(8,128)(2,1)}, bf16[336,1024]{1,0:T(8,128)(2,1)}, u32[]{:S(2)}, u32[]{:S(2)}) %collective-permute-start.2) | collective-permute-done | bytes 688160 | tf_op jit(solution)/shard_map/exchange_keys/ppermute | solution.py:27
  49.1 1.3 collective-permute-start.3
  50.4 18.5 %attend_near.1 = (f32[4,2,96,512]{3,2,1,0:T(8,128)}, f32[4,2,512]{2,1,0:T(2,128)}) custom-call(s32[2]{0:T(128)} %pad_add_fusion.1.par_ref.place, bf16[160,1024]{1,0:T(8,128)(2,1)} %get-tuple-element.21.refs_0_.refs_1_, bf16[160,1024]{1,0:T(8,128)(2,1)} %copy-done.10, bf16[336,1024]{1,0:T(8,128)(2,1)} %get-tuple-element.25.refs_2_.refs_3_.refs_4_, ...), custom_call_target="tpu_custom_call" | custom-call | flops 8000000000 | bytes 4000000 | tf_op jit(solution)/shard_map/attention/attend_near/pallas_call | solution.py:221
  68.8 0.0 collective-permute-done.3.refs_5_
  68.8 0.1 collective-permute-start.20
  68.9 0.0 copy-start.7
  68.9 6.2 %attend_far.1 = bf16[4,160,512]{2,1,0:T(8,128)(2,1)} custom-call(s32[2]{0:T(128)} %pad_add_fusion.1.par_ref.place, bf16[160,1024]{1,0:T(8,128)(2,1)} %get-tuple-element.21.refs_0_.refs_1_, bf16[160,1024]{1,0:T(8,128)(2,1)} %copy-done.10, bf16[336,1024]{1,0:T(8,128)(2,1)} %get-tuple-element.25.refs_2_.refs_3_.refs_4_, ...), custom_call_target="tpu_custom_call" | custom-call | flops 4000000000 | bytes 4000000 | tf_op jit(solution)/shard_map/attention/attend_far/pallas_call | solution.py:221
  75.1 1.0 slice_bitcast_fusion.1
  76.1 0.0 copy-start.1
  76.1 0.7 collective-permute-start.7
  76.8 1.5 collective-permute-start.9
  78.3 1.0 slice.34
  79.3 3.7 %collective-permute-done.9.refs_4_ = bf16[160,512]{1,0:T(8,128)(2,1)S(1)} collective-permute-done((bf16[160,512]{1,0:T(8,128)(2,1)S(1)}, bf16[160,512]{1,0:T(8,128)(2,1)S(1)}, u32[]{:S(2)}, u32[]{:S(2)}) %collective-permute-start.9) | collective-permute-done | bytes 163872 | tf_op jit(solution)/shard_map/exchange_context/ppermute | solution.py:21
  83.0 0.7 copy-done.2
  83.7 1.5 collective-permute-start.6
  85.2 7.3 %collective-permute-done.6 = bf16[2,160,512]{2,1,0:T(8,128)(2,1)S(1)} collective-permute-done((bf16[2,160,512]{2,1,0:T(8,128)(2,1)S(1)}, bf16[2,160,512]{2,1,0:T(8,128)(2,1)S(1)}, u32[]{:S(2)}, u32[]{:S(2)}) %collective-permute-start.6) | collective-permute-done | bytes 327712 | tf_op jit(solution)/shard_map/exchange_context/ppermute | solution.py:21
  92.5 0.7 slice_bitcast_fusion
  93.3 5.8 %collective-permute-done.11.refs_6_ = bf16[160,512]{1,0:T(8,128)(2,1)} collective-permute-done((bf16[160,512]{1,0:T(8,128)(2,1)S(1)}, bf16[160,512]{1,0:T(8,128)(2,1)}, u32[]{:S(2)}, u32[]{:S(2)}) %collective-permute-start.11) | collective-permute-done | bytes 163872 | tf_op jit(solution)/shard_map/exchange_context/ppermute | solution.py:21
  99.0 0.1 collective-permute-start.8
  99.2 0.6 collective-permute-start.10
  99.7 1.1 collective-permute-done.8.refs_3_
  100.8 0.4 collective-permute-start.12
  101.2 0.6 reshape.55.refs_9_
  101.8 0.6 pad_add_fusion.place
  102.4 4.1 %collective-permute-done.10.refs_5_ = bf16[160,512]{1,0:T(8,128)(2,1)} collective-permute-done((bf16[160,512]{1,0:T(8,128)(2,1)}, bf16[160,512]{1,0:T(8,128)(2,1)}, u32[]{:S(2)}, u32[]{:S(2)}) %collective-permute-start.10) | collective-permute-done | bytes 163872 | tf_op jit(solution)/shard_map/exchange_context/ppermute | solution.py:21
  106.5 2.4 %collective-permute-done.12.refs_7_ = bf16[160,512]{1,0:T(8,128)(2,1)} collective-permute-done((bf16[160,512]{1,0:T(8,128)(2,1)}, bf16[160,512]{1,0:T(8,128)(2,1)}, u32[]{:S(2)}, u32[]{:S(2)}) %collective-permute-start.12) | collective-permute-done | bytes 163872 | tf_op jit(solution)/shard_map/exchange_context/ppermute | solution.py:21
  108.9 12.5 %mixer.3 = (bf16[256,1280]{1,0:T(8,128)(2,1)}, f32[256,1280]{1,0:T(8,128)}) custom-call(s32[4]{0:T(128)} %pad_add_fusion.place, bf16[160,512]{1,0:T(8,128)(2,1)} %copy-done.1, bf16[160,512]{1,0:T(8,128)(2,1)} %get-tuple-element.40.refs_1_, bf16[160,512]{1,0:T(8,128)(2,1)} %collective-permute-done.7.refs_2_, bf16[160,512]{1,0:T(8,128)(2,1)} %collective-permute-done.8.refs_3_, ...), custom_call_target="tpu_custom_call" | custom-call | flops 5000000000 | bytes 20000000 | tf_op jit(solution)/shard_map/mixer/mixer/pallas_call | solution.py:297
  121.4 0.0 copy-start.6
  121.4 0.0 copy-start.8
  121.4 0.0 copy-start.9
  121.4 0.9 collective-permute-start.19
  122.3 12.4 %mixer.2 = (bf16[256,1280]{1,0:T(8,128)(2,1)}, f32[256,1280]{1,0:T(8,128)}) custom-call(s32[4]{0:T(128)} %pad_add_fusion.place, bf16[160,512]{1,0:T(8,128)(2,1)} %copy-done.1, bf16[160,512]{1,0:T(8,128)(2,1)} %get-tuple-element.40.refs_1_, bf16[160,512]{1,0:T(8,128)(2,1)} %collective-permute-done.7.refs_2_, bf16[160,512]{1,0:T(8,128)(2,1)} %collective-permute-done.8.refs_3_, ...), custom_call_target="tpu_custom_call" | custom-call | flops 5000000000 | bytes 20000000 | tf_op jit(solution)/shard_map/mixer/mixer/pallas_call | solution.py:297
  134.8 1.3 collective-permute-start.18
  136.1 0.8 reduce-window.6
  136.8 0.2 slice_reduce_fusion
  137.1 0.6 reshape.56.gain_ref
  137.7 0.6 subtract_bitcast_fusion.index_ref
  138.3 1.0 collective-permute-done.19.received
  139.3 0.9 copy-done.4
  140.2 4.8 %gather.1.earlier = bf16[4,256,1280]{2,1,0:T(8,128)(2,1)} custom-call(s32[4]{0:T(128)} %pad_add_fusion.place, s32[4,256]{1,0:T(4,128)} %subtract_bitcast_fusion.index_ref, f32[256,1280]{1,0:T(8,128)} %get-tuple-element.33.kept, bf16[256,1280]{1,0:T(8,128)(2,1)} %copy-done.4, f32[1,1280]{1,0:T(1,128)} %reshape.56.gain_ref), custom_call_target="tpu_custom_call" | custom-call | flops 1000000000 | bytes 5000000 | tf_op jit(solution)/shard_map/merge/gather/pallas_call | solution.py:347
  145.0 7.7 %collective-permute-done.18.received = bf16[256,1280]{1,0:T(8,128)(2,1)S(1)} collective-permute-done((bf16[256,1280]{1,0:T(8,128)(2,1)}, bf16[256,1280]{1,0:T(8,128)(2,1)S(1)}, u32[]{:S(2)}, u32[]{:S(2)}) %collective-permute-start.18) | collective-permute-done | bytes 655392 | tf_op jit(solution)/shard_map/mixer/ppermute | solution.py:21
  152.8 0.8 copy-done.3
  153.6 9.7 %merge.1 = (f32[256,320]{1,0:T(8,128)}, f32[256,320]{1,0:T(8,128)}) custom-call(s32[4]{0:T(128)} %pad_add_fusion.place, s32[4,256]{1,0:T(4,128)} %subtract_bitcast_fusion.index_ref, f32[256,1280]{1,0:T(8,128)} %get-tuple-element.31.kept, bf16[256,1280]{1,0:T(8,128)(2,1)} %copy-done.3, f32[1,1280]{1,0:T(1,128)} %reshape.56.gain_ref, ...), custom_call_target="tpu_custom_call" | custom-call | flops 3000000000 | bytes 12000000 | tf_op jit(solution)/shard_map/merge/merge/pallas_call | solution.py:383
  163.3 0.1 fusion
  163.4 0.6 bitcast_add_fusion.position
  164.0 1.2 collective-permute-done.21.received
  165.2 0.8 copy-done.5
  166.0 2.2 %place.1 = bf16[512,320]{1,0:T(8,128)(2,1)} custom-call(s32[1,256]{1,0:T(1,128)} %bitcast_add_fusion.position, f32[256,320]{1,0:T(8,128)} %get-tuple-element.35.own, f32[256,320]{1,0:T(8,128)} %copy-done.5), custom_call_target="tpu_custom_call" | custom-call | tf_op jit(solution)/shard_map/place/place/pallas_call | solution.py:519
  168.1 21.0 %all_to_all.5 = bf16[8,64,320]{2,1,0:T(8,128)(2,1)S(1)} all-to-all(bf16[8,64,320]{2,1,0:T(8,128)(2,1)} %bitcast.41), channel_id=1, replica_groups=mesh['req'=8,'tp'=4] {'req'}, dimensions={0} | all-to-all | bytes 655360 | tf_op jit(solution)/shard_map/place/all_to_all | solution.py:525
  189.2 0.7 copy.14
  (29 shorter events, 0.1 us)
Async XLA Ops:
  0.0 19.8 %copy-start = (bf16[1280,1280]{1,0:T(8,128)(2,1)S(1)}, bf16[1280,1280]{1,0:T(8,128)(2,1)}, u32[]{:S(2)}) copy-start(bf16[1280,1280]{1,0:T(8,128)(2,1)} %refs_14_.3) | copy-start | bytes 9830404
  12.5 18.7 %collective-permute-start = (bf16[336,1024]{1,0:T(8,128)(2,1)}, bf16[336,1024]{1,0:T(8,128)(2,1)}, u32[]{:S(2)}, u32[]{:S(2)}) collective-permute-start(bf16[336,1024]{1,0:T(8,128)(2,1)} %get-tuple-element.23), channel_id=1, source_target_pairs={{0,4},{4,0},{8,12},{12,8},{16,20},{20,16},{24,28},{28,24},{1,5},{5... | collective-permute-start | bytes 2064392 | tf_op jit(solution)/shard_map/exchange_keys/ppermute | solution.py:21
  15.5 20.3 %collective-permute-start.4 = (bf16[336,1024]{1,0:T(8,128)(2,1)}, bf16[336,1024]{1,0:T(8,128)(2,1)}, u32[]{:S(2)}, u32[]{:S(2)}) collective-permute-start(bf16[336,1024]{1,0:T(8,128)(2,1)} %get-tuple-element.25.refs_2_.refs_3_.refs_4_), channel_id=1, source_target_pairs={{0,8},{4,12},{8,16},{12,20},{16,24},{20,28},{1,9},{5,13},{9,17},{1... | collective-permute-start | bytes 2064392 | tf_op jit(solution)/shard_map/exchange_keys/ppermute | solution.py:27
  19.8 89.1 %collective-permute-start.16 = (bf16[1280,1280]{1,0:T(8,128)(2,1)S(1)}, bf16[1280,1280]{1,0:T(8,128)(2,1)}, u32[]{:S(2)}, u32[]{:S(2)}) collective-permute-start(bf16[1280,1280]{1,0:T(8,128)(2,1)S(1)} %copy-done), channel_id=1, source_target_pairs={{0,1},{1,0},{2,3},{3,2},{4,5},{5,4},{6,7},{7,6},{8,9},{9,8},{10,11... | collective-permute-start | bytes 9830408 | tf_op jit(solution)/shard_map/weights/ppermute | solution.py:21
  19.8 89.1 %collective-permute-start.17 = (bf16[1280,1280]{1,0:T(8,128)(2,1)}, bf16[1280,1280]{1,0:T(8,128)(2,1)}, u32[]{:S(2)}, u32[]{:S(2)}) collective-permute-start(bf16[1280,1280]{1,0:T(8,128)(2,1)} %refs_16_.3), channel_id=1, source_target_pairs={{0,1},{1,0},{2,3},{3,2},{4,5},{5,4},{6,7},{7,6},{8,9},{9,8},{10,11... | collective-permute-start | bytes 9830408 | tf_op jit(solution)/shard_map/weights/ppermute | solution.py:21
  20.3 24.7 %collective-permute-start.5 = (bf16[336,1024]{1,0:T(8,128)(2,1)}, bf16[336,1024]{1,0:T(8,128)(2,1)}, u32[]{:S(2)}, u32[]{:S(2)}) collective-permute-start(bf16[336,1024]{1,0:T(8,128)(2,1)} %get-tuple-element.25.refs_2_.refs_3_.refs_4_), channel_id=1, source_target_pairs={{8,0},{12,4},{16,8},{20,12},{24,16},{28,20},{9,1},{13,5},{17,9},{2... | collective-permute-start | bytes 2064392 | tf_op jit(solution)/shard_map/exchange_keys/ppermute | solution.py:27
  31.2 17.8 %collective-permute-start.2 = (bf16[336,1024]{1,0:T(8,128)(2,1)}, bf16[336,1024]{1,0:T(8,128)(2,1)}, u32[]{:S(2)}, u32[]{:S(2)}) collective-permute-start(bf16[336,1024]{1,0:T(8,128)(2,1)} %collective-permute-done.refs_3_.refs_5_), channel_id=1, source_target_pairs={{0,8},{4,12},{8,16},{12,20},{16,24},{20,28},{1,9},{5,13},{9,17},{1... | collective-permute-start | bytes 2064392 | tf_op jit(solution)/shard_map/exchange_keys/ppermute | solution.py:27
  35.8 9.3 %collective-permute-start.1 = (bf16[160,1024]{1,0:T(8,128)(2,1)}, bf16[160,1024]{1,0:T(8,128)(2,1)S(1)}, u32[]{:S(2)}, u32[]{:S(2)}) collective-permute-start(bf16[160,1024]{1,0:T(8,128)(2,1)} %get-tuple-element.24), channel_id=1, source_target_pairs={{0,4},{4,0},{8,12},{12,8},{16,20},{20,16},{24,28},{28,24},{1,5},{5... | collective-permute-start | bytes 983048 | tf_op jit(solution)/shard_map/exchange_keys/ppermute | solution.py:21
  45.0 31.1 %collective-permute-start.13 = (bf16[2,160,1280]{2,1,0:T(8,128)(2,1)}, bf16[2,160,1280]{2,1,0:T(8,128)(2,1)}, u32[]{:S(2)}, u32[]{:S(2)}) collective-permute-start(bf16[2,160,1280]{2,1,0:T(8,128)(2,1)} %bitcast.35), channel_id=1, source_target_pairs={{0,1},{1,0},{2,3},{3,2},{4,5},{5,4},{6,7},{7,6},{8,9},{9,8},{10,11... | collective-permute-start | bytes 2457608 | tf_op jit(solution)/shard_map/weights/ppermute | solution.py:21
  45.1 5.2 %copy-start.10 = (bf16[160,1024]{1,0:T(8,128)(2,1)}, bf16[160,1024]{1,0:T(8,128)(2,1)S(1)}, u32[]{:S(2)}) copy-start(bf16[160,1024]{1,0:T(8,128)(2,1)S(1)} %collective-permute-done.1.refs_1_) | copy-start | bytes 983044
  45.1 31.7 %collective-permute-start.14 = (bf16[2,160,1280]{2,1,0:T(8,128)(2,1)}, bf16[2,160,1280]{2,1,0:T(8,128)(2,1)}, u32[]{:S(2)}, u32[]{:S(2)}) collective-permute-start(bf16[2,160,1280]{2,1,0:T(8,128)(2,1)} %bitcast.36), channel_id=1, source_target_pairs={{0,2},{1,3},{2,0},{3,1},{4,6},{5,7},{6,4},{7,5},{8,10},{9,11},{10,... | collective-permute-start | bytes 2457608 | tf_op jit(solution)/shard_map/weights/ppermute | solution.py:21
  49.1 19.8 %collective-permute-start.3 = (bf16[336,1024]{1,0:T(8,128)(2,1)}, bf16[336,1024]{1,0:T(8,128)(2,1)}, u32[]{:S(2)}, u32[]{:S(2)}) collective-permute-start(bf16[336,1024]{1,0:T(8,128)(2,1)} %collective-permute-done.refs_3_.refs_5_), channel_id=1, source_target_pairs={{8,0},{12,4},{16,8},{20,12},{24,16},{28,20},{9,1},{13,5},{17,9},{2... | collective-permute-start | bytes 2064392 | tf_op jit(solution)/shard_map/exchange_keys/ppermute | solution.py:27
  68.8 76.2 %collective-permute-start.20 = (bf16[320,5120]{1,0:T(8,128)(2,1)}, bf16[320,5120]{1,0:T(8,128)(2,1)}, u32[]{:S(2)}, u32[]{:S(2)}) collective-permute-start(bf16[320,5120]{1,0:T(8,128)(2,1)} %bitcast.33), channel_id=1, source_target_pairs={{0,1},{1,0},{2,3},{3,2},{4,5},{5,4},{6,7},{7,6},{8,9},{9,8},{10,11... | collective-permute-start | bytes 9830408 | tf_op jit(solution)/shard_map/weights/ppermute | solution.py:21
  68.9 32.3 %copy-start.7 = (bf16[1280]{0:T(1024)(128)(2,1)S(1)}, bf16[1280]{0:T(1024)(128)(2,1)}, u32[]{:S(2)}) copy-start(bf16[1280]{0:T(1024)(128)(2,1)} %param.17) | copy-start | bytes 7684
  76.1 32.8 %copy-start.1 = (bf16[160,512]{1,0:T(8,128)(2,1)}, bf16[160,512]{1,0:T(8,128)(2,1)S(1)}, u32[]{:S(2)}) copy-start(bf16[160,512]{1,0:T(8,128)(2,1)S(1)} %get-tuple-element.38.refs_0_) | copy-start | bytes 491524
  76.1 2.2 %collective-permute-start.7 = (bf16[160,512]{1,0:T(8,128)(2,1)S(1)}, bf16[160,512]{1,0:T(8,128)(2,1)}, u32[]{:S(2)}, u32[]{:S(2)}) collective-permute-start(bf16[160,512]{1,0:T(8,128)(2,1)S(1)} %get-tuple-element.37), channel_id=1, source_target_pairs={{0,1},{1,0},{2,3},{3,2},{4,5},{5,4},{6,7},{7,6},{8,9},{9,8},{10,11... | collective-permute-start | bytes 491528 | tf_op jit(solution)/shard_map/exchange_context/ppermute | solution.py:21
  76.8 6.2 %collective-permute-start.9 = (bf16[160,512]{1,0:T(8,128)(2,1)S(1)}, bf16[160,512]{1,0:T(8,128)(2,1)S(1)}, u32[]{:S(2)}, u32[]{:S(2)}) collective-permute-start(bf16[160,512]{1,0:T(8,128)(2,1)S(1)} %get-tuple-element.38.refs_0_), channel_id=1, source_target_pairs={{0,2},{1,3},{2,0},{3,1},{4,6},{5,7},{6,4},{7,5},{8,10},{9,11},{10,... | collective-permute-start | bytes 491528 | tf_op jit(solution)/shard_map/exchange_context/ppermute | solution.py:21
  78.3 20.8 %collective-permute-start.15 = (bf16[2,160,1280]{2,1,0:T(8,128)(2,1)}, bf16[2,160,1280]{2,1,0:T(8,128)(2,1)}, u32[]{:S(2)}, u32[]{:S(2)}) collective-permute-start(bf16[2,160,1280]{2,1,0:T(8,128)(2,1)} %collective-permute-done.14.refs_12_), channel_id=1, source_target_pairs={{0,1},{1,0},{2,3},{3,2},{4,5},{5,4},{6,7},{7,6},{8,9},{9,8},{10,11... | collective-permute-start | bytes 2457608 | tf_op jit(solution)/shard_map/weights/ppermute | solution.py:21
  83.0 0.7 copy-start.2
  83.7 8.9 %collective-permute-start.6 = (bf16[2,160,512]{2,1,0:T(8,128)(2,1)S(1)}, bf16[2,160,512]{2,1,0:T(8,128)(2,1)S(1)}, u32[]{:S(2)}, u32[]{:S(2)}) collective-permute-start(bf16[2,160,512]{2,1,0:T(8,128)(2,1)S(1)} %slice.34), channel_id=1, source_target_pairs={{0,4},{4,0},{8,12},{12,8},{16,20},{20,16},{24,28},{28,24},{1,5},{5... | collective-permute-start | bytes 983048 | tf_op jit(solution)/shard_map/exchange_context/ppermute | solution.py:21
  92.5 6.5 %collective-permute-start.11 = (bf16[160,512]{1,0:T(8,128)(2,1)S(1)}, bf16[160,512]{1,0:T(8,128)(2,1)}, u32[]{:S(2)}, u32[]{:S(2)}) collective-permute-start(bf16[160,512]{1,0:T(8,128)(2,1)S(1)} %get-tuple-element.37), channel_id=1, source_target_pairs={{0,3},{1,2},{2,1},{3,0},{4,7},{5,6},{6,5},{7,4},{8,11},{9,10},{10,... | collective-permute-start | bytes 491528 | tf_op jit(solution)/shard_map/exchange_context/ppermute | solution.py:21
  99.0 1.7 collective-permute-start.8
  99.2 7.4 %collective-permute-start.10 = (bf16[160,512]{1,0:T(8,128)(2,1)}, bf16[160,512]{1,0:T(8,128)(2,1)}, u32[]{:S(2)}, u32[]{:S(2)}) collective-permute-start(bf16[160,512]{1,0:T(8,128)(2,1)} %get-tuple-element.40.refs_1_), channel_id=1, source_target_pairs={{0,2},{1,3},{2,0},{3,1},{4,6},{5,7},{6,4},{7,5},{8,10},{9,11},{10,... | collective-permute-start | bytes 491528 | tf_op jit(solution)/shard_map/exchange_context/ppermute | solution.py:21
  100.8 8.2 %collective-permute-start.12 = (bf16[160,512]{1,0:T(8,128)(2,1)}, bf16[160,512]{1,0:T(8,128)(2,1)}, u32[]{:S(2)}, u32[]{:S(2)}) collective-permute-start(bf16[160,512]{1,0:T(8,128)(2,1)} %get-tuple-element.39), channel_id=1, source_target_pairs={{0,3},{1,2},{2,1},{3,0},{4,7},{5,6},{6,5},{7,4},{8,11},{9,10},{10,... | collective-permute-start | bytes 491528 | tf_op jit(solution)/shard_map/exchange_context/ppermute | solution.py:21
  121.4 14.6 %copy-start.6 = (s32[256,1]{0,1:T(1,128)S(1)}, s32[256,1]{0,1:T(1,128)}, u32[]{:S(2)}) copy-start(s32[256,1]{0,1:T(1,128)} %param.23) | copy-start | bytes 3076
  121.4 15.7 %copy-start.8 = (bf16[1280]{0:T(1024)(128)(2,1)S(1)}, bf16[1280]{0:T(1024)(128)(2,1)}, u32[]{:S(2)}) copy-start(bf16[1280]{0:T(1024)(128)(2,1)} %param.20) | copy-start | bytes 7684
  121.4 16.3 %copy-start.9 = (s32[256,4]{0,1:T(4,128)S(1)}, s32[256,4]{0,1:T(4,128)}, u32[]{:S(2)}) copy-start(s32[256,4]{0,1:T(4,128)} %param.22) | copy-start | bytes 12292
  121.4 17.8 %collective-permute-start.19 = (bf16[256,1280]{1,0:T(8,128)(2,1)}, bf16[256,1280]{1,0:T(8,128)(2,1)S(1)}, u32[]{:S(2)}, u32[]{:S(2)}) collective-permute-start(bf16[256,1280]{1,0:T(8,128)(2,1)} %get-tuple-element.34), channel_id=1, source_target_pairs={{0,2},{1,3},{2,0},{3,1},{4,6},{5,7},{6,4},{7,5},{8,10},{9,11},{10,... | collective-permute-start | bytes 1966088 | tf_op jit(solution)/shard_map/mixer/ppermute | solution.py:21
  134.8 18.0 %collective-permute-start.18 = (bf16[256,1280]{1,0:T(8,128)(2,1)}, bf16[256,1280]{1,0:T(8,128)(2,1)S(1)}, u32[]{:S(2)}, u32[]{:S(2)}) collective-permute-start(bf16[256,1280]{1,0:T(8,128)(2,1)} %get-tuple-element.32), channel_id=1, source_target_pairs={{0,2},{1,3},{2,0},{3,1},{4,6},{5,7},{6,4},{7,5},{8,10},{9,11},{10,... | collective-permute-start | bytes 1966088 | tf_op jit(solution)/shard_map/mixer/ppermute | solution.py:21
  139.3 0.9 copy-start.4
  152.8 0.8 copy-start.3
  163.3 1.9 %collective-permute-start.21 = (f32[256,320]{1,0:T(8,128)}, f32[256,320]{1,0:T(8,128)S(1)}, u32[]{:S(2)}, u32[]{:S(2)}) collective-permute-start(f32[256,320]{1,0:T(8,128)} %get-tuple-element.36), channel_id=1, source_target_pairs={{0,1},{1,0},{2,3},{3,2},{4,5},{5,4},{6,7},{7,6},{8,9},{9,8},{10,11... | collective-permute-start | bytes 983048 | tf_op jit(solution)/shard_map/merge/ppermute | solution.py:21
  165.2 0.8 copy-start.5

commit v2 on v1

v2 whole, which is shorter than its diff:
```python
import functools
import math

import jax
import jax.numpy as jnp
from jax import lax
from jax.experimental import pallas as pl
from jax.experimental.pallas import tpu as pltpu
from jax.sharding import PartitionSpec as P

HD = 80
TILE = 512
MASKED = -1e30
START = -1e28
FACTOR = 1.0 / math.sqrt(HD)
SEGMENT_ROWS = 16
VROWS = 96
LANES = 256
AHEAD = 2
SMALL = 60.0


def swap(block, axis, flip):
    return lax.ppermute(block, axis, [(i, i ^ flip) for i in range(lax.axis_size(axis))])


def shifted(block, axis, distance):
    devices = range(lax.axis_size(axis))
    route = [(i - distance, i) for i in devices if i - distance in devices]
    return lax.ppermute(block, axis, route)


def normalized(stream, gain):
    center = jnp.mean(stream, axis=-1, keepdims=True)
    moved = stream - center
    spread = jnp.mean(moved * moved, axis=-1, keepdims=True)
    return (moved * lax.rsqrt(spread + 1e-06) * gain).astype(jnp.bfloat16)


def dot(a, b, contract):
    return lax.dot_general(a, b, (contract, ((), ())), preferred_element_type=jnp.float32)


NN = ((1,), (0,))
NT = ((1,), (1,))


def row_of(gain_ref):
    return gain_ref[...].astype(jnp.float32).reshape(1, gain_ref.shape[0])


def vmem():
    return pltpu.CompilerParams(vmem_limit_bytes=60 << 20)


def project_kernel(x_ref, segment_ref, gain_ref, w_ref, kv_keep, kv_send, q_keep, q_send):
    first = lax.axis_index("req") % 2 == 0
    half = q_keep.shape[0]
    rows = normalized(x_ref[...].astype(jnp.float32), row_of(gain_ref))
    number = segment_ref[...] + 1
    row = lax.broadcasted_iota(jnp.int32, (SEGMENT_ROWS, 1), 0)
    number = jnp.where(row == 0, number & 255, jnp.where(row == 1, number >> 8, 0))
    number = number.astype(jnp.float32).astype(jnp.bfloat16)
    out = dot(w_ref[...], rows, NT)
    for part, keep, send in ((0, q_keep, q_send), (1, kv_keep, kv_send), (2, kv_keep, kv_send)):
        low = out[2 * part * half : (2 * part + 1) * half]
        high = out[(2 * part + 1) * half : (2 * part + 2) * half]
        at = slice(max(part - 1, 0) * half, max(part, 1) * half)
        keep[at, :] = jnp.where(first, low, high).astype(jnp.bfloat16)
        send[at, :] = jnp.where(first, high, low).astype(jnp.bfloat16)
    kv_keep[2 * half :, :] = number
    kv_send[2 * half :, :] = number


def project(tokens, segments, gain, weight):
    rows, width = tokens.shape
    half = weight.shape[0] // 6
    step = 256
    tall = 2 * half + SEGMENT_ROWS
    shapes = [(tall, rows), (tall, rows), (half, rows), (half, rows)]
    return pl.pallas_call(
        project_kernel,
        grid=(rows // step,),
        in_specs=[
            pl.BlockSpec((step, width), lambda i: (i, 0)),
            pl.BlockSpec((1, step), lambda i: (0, i)),
            pl.BlockSpec(gain.shape, lambda i: (0,)),
            pl.BlockSpec(weight.shape, lambda i: (0, 0)),
        ],
        out_specs=[pl.BlockSpec((s[0], step), lambda i: (0, i)) for s in shapes],
        out_shape=[jax.ShapeDtypeStruct(s, jnp.bfloat16) for s in shapes],
        compiler_params=vmem(),
        name="project",
    )(tokens, segments, gain, weight)


def numbers_of(ref, at):
    two = ref[:, at].astype(jnp.float32)
    return two[0:1] + 256.0 * two[1:2]


def largest_norm(first, second):
    squares = []
    for block in (first, second):
        block = block.astype(jnp.float32)
        squares.append(jnp.sum(block * block, axis=0, keepdims=True))
    return jnp.max(jnp.maximum(squares[0], squares[1]))


def attend_kernel(blocks, resumed, last, place, q_ref, number_ref, *refs):
    kv_refs, refs = refs[:blocks], refs[blocks:]
    if resumed:
        acc_in, peak_in, refs = refs[0], refs[1], refs[2:]
    if last:
        ctx_out, refs = refs[0], refs[1:]
    else:
        acc_out, peak_out, refs = refs[0], refs[1], refs[2:]
    keys, values, columns, acc, peak, bounds, plain = refs
    tiles_of = kv_refs[0].shape[1] // TILE
    tiles = blocks * tiles_of
    tall = kv_refs[0].shape[0] - SEGMENT_ROWS

    @pl.when(pl.program_id(0) == 0)
    def _():
        for b in range(blocks):
            for t in range(tiles_of):
                n = b * tiles_of + t
                at = slice(t * TILE, (t + 1) * TILE)
                for h in range(2):
                    block = kv_refs[b][h * HD : (h + 1) * HD, at].astype(jnp.float32)
                    keys[n, h] = jnp.transpose(block).astype(jnp.bfloat16)
                    values[n, h, :HD] = kv_refs[b][(2 + h) * HD : (3 + h) * HD, at]
                    values[n, h, HD:] = jnp.ones((VROWS - HD, TILE), jnp.bfloat16)
                number = numbers_of(kv_refs[b].at[tall:], at)
                bounds[3 * n] = jnp.min(number)
                bounds[3 * n + 1] = jnp.max(number)
                bounds[3 * n + 2] = largest_norm(kv_refs[b][:HD, at], kv_refs[b][HD : 2 * HD, at])
                columns[n] = jnp.transpose(jnp.broadcast_to(number, (128, TILE)))

    if resumed:
        acc[...] = acc_in[0]
        peak[...] = peak_in[0]
        plain[0] = (jnp.max(jnp.abs(peak_in[0])) == 0.0).astype(jnp.int32)
    else:
        acc[...] = jnp.zeros_like(acc)
        peak[...] = jnp.zeros_like(peak)
        plain[0] = 1

    q_row = numbers_of(number_ref, slice(0, TILE))
    q_low, q_high = jnp.min(q_row), jnp.max(q_row)
    q_norm = largest_norm(q_ref[:HD, :], q_ref[HD:, :])

    def scores_of(t, h, at, matches):
        scores = dot(keys[t, h], q_ref[h * HD : (h + 1) * HD, at], NN)
        return scores if matches is None else jnp.where(matches, scores, MASKED)

    def matches_of(t, at):
        column = columns[t]
        return jnp.concatenate([column] * (LANES // 128), axis=1) == q_row[:, at]

    units = [(slice(c, c + LANES), h) for c in range(0, TILE, LANES) for h in range(2)]

    def unshifted(t, masked):
        scores, probs, matches = {}, {}, None
        for i in range(len(units) + AHEAD + 1):
            if i < len(units):
                at, h = units[i]
                if masked and h == 0:
                    matches = matches_of(t, at)
                scores[i] = scores_of(t, h, at, matches)
            if 0 <= i - AHEAD < len(units):
                probs[i - AHEAD] = jnp.exp(scores.pop(i - AHEAD) * FACTOR).astype(jnp.bfloat16)
            if 0 <= i - AHEAD - 1 < len(units):
                at, h = units[i - AHEAD - 1]
                acc[h, :, at] += dot(values[t, h], probs.pop(i - AHEAD - 1), NN)

    def shifted_by_peak(t):
        for at, h in units:
            scores = scores_of(t, h, at, matches_of(t, at))
            old = jnp.where(acc[h, HD : HD + 1, at] > 0.0, peak[h : h + 1, at], START)
            new = jnp.maximum(old, jnp.max(scores, axis=0, keepdims=True))
            probs = jnp.exp((scores - new) * FACTOR).astype(jnp.bfloat16)
            shrink = jnp.exp((old - new) * FACTOR)
            peak[h : h + 1, at] = new
            acc[h, :, at] = acc[h, :, at] * shrink + dot(values[t, h], probs, NN)
        plain[0] = 0

    def visit(t, carry):
        k_low, k_high = bounds[3 * t], bounds[3 * t + 1]
        touches = (k_high >= q_low) & (k_low <= q_high)
        whole = (k_low == k_high) & (q_low == q_high)
        small = (plain[0] == 1) & (q_norm * bounds[3 * t + 2] <= SMALL * SMALL * HD)

        @pl.when(touches & small & whole)
        def _():
            unshifted(t, False)

        @pl.when(touches & small & jnp.logical_not(whole))
        def _():
            unshifted(t, True)

        @pl.when(touches & jnp.logical_not(small))
        def _():
            shifted_by_peak(t)

        return carry

    lax.fori_loop(0, tiles, visit, 0)
    if last:
        for h in range(2):
            at = slice(h * HD, (h + 1) * HD)
            ctx_out[0, at, :] = (acc[h, :HD] / acc[h, HD : HD + 1]).astype(jnp.bfloat16)
    else:
        acc_out[0] = acc[...]
        peak_out[0] = peak[...]


def attend(place, queries, numbers, key_values, name, state=None, last=False):
    half, rows = queries.shape
    steps = rows // TILE
    blocks = len(key_values)
    tiles = blocks * steps
    tall = numbers.shape[0] - SEGMENT_ROWS
    whole = lambda a: pl.BlockSpec(a.shape, lambda j, s: (0,) * a.ndim)
    acc_shape, peak_shape = (2, VROWS, TILE), (2, TILE)
    acc_spec = pl.BlockSpec((1,) + acc_shape, lambda j, s: (j, 0, 0, 0))
    peak_spec = pl.BlockSpec((1,) + peak_shape, lambda j, s: (j, 0, 0))
    in_specs = [
        pl.BlockSpec((half, TILE), lambda j, s: (0, j ^ s[1])),
        pl.BlockSpec((SEGMENT_ROWS, TILE), lambda j, s: (tall // SEGMENT_ROWS, j ^ s[1])),
    ] + [whole(kv) for kv in key_values]
    operands = [queries, numbers, *key_values]
    if state is not None:
        in_specs += [acc_spec, peak_spec]
        operands += list(state)
    if last:
        out_specs = pl.BlockSpec((1, half, TILE), lambda j, s: (j, 0, 0))
        out_shape = jax.ShapeDtypeStruct((steps, half, TILE), jnp.bfloat16)
    else:
        out_specs = [acc_spec, peak_spec]
        out_shape = [
            jax.ShapeDtypeStruct((steps,) + acc_shape, jnp.float32),
            jax.ShapeDtypeStruct((steps,) + peak_shape, jnp.float32),
        ]
    return pl.pallas_call(
        functools.partial(attend_kernel, blocks, state is not None, last),
        grid_spec=pltpu.PrefetchScalarGridSpec(
            num_scalar_prefetch=1,
            grid=(steps,),
            in_specs=in_specs,
            out_specs=out_specs,
            scratch_shapes=[
                pltpu.VMEM((tiles, 2, TILE, HD), jnp.bfloat16),
                pltpu.VMEM((tiles, 2, VROWS, TILE), jnp.bfloat16),
                pltpu.VMEM((tiles, TILE, 128), jnp.float32),
                pltpu.VMEM(acc_shape, jnp.float32),
                pltpu.VMEM(peak_shape, jnp.float32),
                pltpu.SMEM((3 * tiles,), jnp.float32),
                pltpu.SMEM((1,), jnp.int32),
            ],
        ),
        out_shape=out_shape,
        compiler_params=vmem(),
        cost_estimate=pl.CostEstimate(
            flops=1_000_000_000 * blocks, bytes_accessed=4_000_000, transcendentals=0
        ),
        name=name,
    )(place, *operands)


def mixer_kernel(place, *refs):
    sources, refs = refs[:8], refs[8:]
    x_ref, gain_ref, refs = refs[0], refs[1], refs[2:]
    wo_hbm, refs = refs[:4], refs[4:]
    (we_own, we_other, wr_own, wr_other, sent, kept, refs) = (*refs[:6], refs[6:])
    context, hidden, wo, we, wr, sems = refs
    par = place[0]
    half = sources[0].shape[1]
    width = we.shape[2]
    copies = []
    for i in range(8):
        copies.append(
            pltpu.make_async_copy(
                wo_hbm[i // 2].at[par ^ (i % 2)], wo.at[pl.ds(i * half, half)], sems.at[i]
            )
        )
    for i, (source, target) in enumerate(
        [(we_own, we.at[0]), (we_other, we.at[1]), (wr_own, wr.at[0]), (wr_other, wr.at[1])]
    ):
        copies.append(pltpu.make_async_copy(source, target, sems.at[8 + i]))
    for copy in copies:
        copy.start()
    for i in range(8):
        context[i * half : (i + 1) * half, :] = sources[i][0].astype(jnp.float32)
    rows = jnp.transpose(context[...]).astype(jnp.bfloat16)
    for i in range(8):
        copies[i].wait()
    total = x_ref[...].astype(jnp.float32) + dot(rows, wo[...], NN)
    rows = normalized(total, row_of(gain_ref))
    for i in range(2):
        copies[8 + i].wait()
        inner = dot(rows, we[i], NN)
        grown = 0.5 * inner * (1.0 + lax.erf(inner * (1.0 / math.sqrt(2.0))))
        hidden[:, i * width : (i + 1) * width] = grown.astype(jnp.bfloat16)
    for i in range(2):
        copies[10 + i].wait()
    out = dot(hidden[:, :width], wr[0], NN) + dot(hidden[:, width:], wr[1], NN)
    sent[...] = out.astype(jnp.bfloat16)
    kept[...] = total + out


def mixer(place, pieces, tokens, gain, wo, weights, chunk, chunk_rows):
    width = tokens.shape[1]
    half, per_core = pieces[0][0].shape[1:]
    chunks = per_core // chunk_rows
    hidden = weights[0].shape[1]
    piece_spec = lambda which: pl.BlockSpec((1, half, chunk_rows), lambda i, s: (which, 0, chunk))
    any_spec = pl.BlockSpec(memory_space=pl.ANY)
    out_spec = pl.BlockSpec((chunk_rows, width), lambda i, s: (0, 0))
    return pl.pallas_call(
        mixer_kernel,
        grid_spec=pltpu.PrefetchScalarGridSpec(
            num_scalar_prefetch=1,
            grid=(1,),
            in_specs=[piece_spec(which) for _, which in pieces]
            + [
                pl.BlockSpec((chunk_rows, width), lambda i, s: (s[1] * chunks + chunk, 0)),
                pl.BlockSpec(gain.shape, lambda i, s: (0,)),
            ]
            + [any_spec] * 8,
            out_specs=[out_spec, out_spec],
            scratch_shapes=[
                pltpu.VMEM((8 * half, chunk_rows), jnp.float32),
                pltpu.VMEM((chunk_rows, 2 * hidden), jnp.bfloat16),
                pltpu.VMEM((8 * half, width), jnp.bfloat16),
                pltpu.VMEM((2,) + weights[0].shape, jnp.bfloat16),
                pltpu.VMEM((2,) + weights[2].shape, jnp.bfloat16),
                pltpu.SemaphoreType.DMA((12,)),
            ],
        ),
        out_shape=[
            jax.ShapeDtypeStruct((chunk_rows, width), jnp.bfloat16),
            jax.ShapeDtypeStruct((chunk_rows, width), jnp.float32),
        ],
        compiler_params=vmem(),
        cost_estimate=pl.CostEstimate(
            flops=5_000_000_000, bytes_accessed=20_000_000, transcendentals=0
        ),
        name="mixer",
    )(place, *[source for source, _ in pieces], tokens, gain, *wo, *weights)


def one_hot_rows(index_ref, k, first, rows):
    column = jnp.transpose(jnp.broadcast_to(index_ref[k : k + 1, :], (128, index_ref.shape[1])))
    lanes = lax.broadcasted_iota(jnp.int32, (1, 128), 1)
    parts = [column == lanes + (first + 128 * n) for n in range(rows // 128)]
    return jnp.concatenate(parts, axis=1).astype(jnp.float32).astype(jnp.bfloat16)


def gather_kernel(place, index_ref, kept, received, gain_ref, merged):
    rows = kept.shape[0]
    final = normalized(kept[...] + received[...].astype(jnp.float32), row_of(gain_ref))
    for k in range(4):
        merged[k] = dot(one_hot_rows(index_ref, k, place[2], rows), final, NN).astype(jnp.bfloat16)


def gather(place, index, kept, received, gain):
    rows, width = kept.shape
    merged_rows = index.shape[1]
    whole = lambda a: pl.BlockSpec(a.shape, lambda i, s: (0,) * a.ndim)
    return pl.pallas_call(
        gather_kernel,
        grid_spec=pltpu.PrefetchScalarGridSpec(
            num_scalar_prefetch=1,
            grid=(1,),
            in_specs=[whole(index), whole(kept), whole(received), whole(gain)],
            out_specs=pl.BlockSpec((4, merged_rows, width), lambda i, s: (0, 0, 0)),
        ),
        out_shape=jax.ShapeDtypeStruct((4, merged_rows, width), jnp.bfloat16),
        compiler_params=vmem(),
        cost_estimate=pl.CostEstimate(
            flops=1_000_000_000, bytes_accessed=5_000_000, transcendentals=0
        ),
        name="gather",
    )(place, index, kept, received, gain)


def merge_kernel(place, index_ref, kept, received, gain_ref, *refs):
    earlier_hbm, w_own, w_other, own, other, earlier, weights, sems = refs
    rows, width = kept.shape
    copies = [pltpu.make_async_copy(earlier_hbm, earlier, sems.at[0])]
    for k in range(4):
        at = pl.ds(k * width, width)
        for i, source in enumerate((w_own, w_other)):
            target = weights.at[k, pl.ds(i * own.shape[1], own.shape[1])]
            copies.append(pltpu.make_async_copy(source.at[:, at], target, sems.at[1 + 2 * k + i]))
    for copy in copies:
        copy.start()
    final = normalized(kept[...] + received[...].astype(jnp.float32), row_of(gain_ref))
    copies[0].wait()
    total = None
    for k in range(4):
        part = dot(one_hot_rows(index_ref, k, place[3], rows), final, NN)
        part = (part + earlier[k].astype(jnp.float32)).astype(jnp.bfloat16)
        copies[1 + 2 * k].wait()
        copies[2 + 2 * k].wait()
        term = dot(part, weights[k], NT)
        total = term if total is None else total + term
    own[...] = total[:, : own.shape[1]]
    other[...] = total[:, own.shape[1] :]


def merge(place, index, kept, received, gain, earlier, w_own, w_other):
    merged_rows = index.shape[1]
    columns = w_own.shape[0]
    width = kept.shape[1]
    whole = lambda a: pl.BlockSpec(a.shape, lambda i, s: (0,) * a.ndim)
    any_spec = pl.BlockSpec(memory_space=pl.ANY)
    out_spec = pl.BlockSpec((merged_rows, columns), lambda i, s: (0, 0))
    return pl.pallas_call(
        merge_kernel,
        grid_spec=pltpu.PrefetchScalarGridSpec(
            num_scalar_prefetch=1,
            grid=(1,),
            in_specs=[whole(a) for a in (index, kept, received, gain)] + [any_spec] * 3,
            out_specs=[out_spec, out_spec],
            scratch_shapes=[
                pltpu.VMEM(earlier.shape, jnp.bfloat16),
                pltpu.VMEM((4, 2 * columns, width), jnp.bfloat16),
                pltpu.SemaphoreType.DMA((9,)),
            ],
        ),
        out_shape=[jax.ShapeDtypeStruct((merged_rows, columns), jnp.float32)] * 2,
        compiler_params=vmem(),
        cost_estimate=pl.CostEstimate(
            flops=3_000_000_000, bytes_accessed=12_000_000, transcendentals=0
        ),
        name="merge",
    )(place, index, kept, received, gain, earlier, w_own, w_other)


def place_kernel(position, own, received, out):
    feature = (own[...] + received[...]).astype(jnp.bfloat16)
    slots = lax.broadcasted_iota(jnp.int32, (out.shape[0], 1), 0)
    chosen = (slots == position[...]).astype(jnp.float32).astype(jnp.bfloat16)
    out[...] = dot(chosen, feature, NN).astype(jnp.bfloat16)


def body(
    tokens,
    segments,
    attend_gain,
    attend_weight,
    output_weight,
    mixer_gain,
    expand_weight,
    reduce_weight,
    output_gain,
    merge_weight,
    merge_index,
    owners,
):
    rows, width = tokens.shape
    head_width = attend_weight.shape[2]
    half = head_width // 2
    peers = lax.axis_size("req")
    req = lax.axis_index("req")
    par = req % 2
    core = lax.axis_index("tp") % 2

    chunk_rows = 256
    per_core = rows // 2
    place = jnp.stack([par, core, core * per_core, core * per_core + chunk_rows])
    with jax.named_scope("project"):
        weight = jnp.transpose(attend_weight, (1, 2, 0)).reshape(6 * half, width)
        kv_own, kv_send, q_own, q_send = project(tokens, segments[None, :], attend_gain, weight)

    with jax.named_scope("exchange_keys"):
        kv_peer = swap(kv_send, "req", 1)
        kv_before = shifted(kv_own, "req", 2)
        kv_after = shifted(kv_own, "req", -2)
        state_own = attend(place, q_own, kv_own, [kv_own], "attend_own")
        q_send, kv_peer, state_own = lax.optimization_barrier((q_send, kv_peer, state_own))
        q_peer = swap(q_send, "req", 1)
        kv_before_peer = shifted(kv_peer, "req", 2)
        kv_after_peer = shifted(kv_peer, "req", -2)

    with jax.named_scope("weights"):
        wo = [output_weight.reshape(2, half, width)]
        wo.append(swap(wo[0], "tp", 1))
        wo.append(swap(wo[0], "tp", 2))
        wo.append(swap(wo[2], "tp", 1))
        expand_other = swap(expand_weight, "tp", 1)
        reduce_other = swap(reduce_weight, "tp", 1)
        merge_own = jnp.transpose(merge_weight)
        merge_other = swap(merge_own, "tp", 1)

    with jax.named_scope("attention"):
        near = [kv_peer, kv_before, kv_after]
        far = [kv_before_peer, kv_after_peer]
        state_own = attend(place, q_own, kv_own, near, "attend_near", state_own)
        state_peer = attend(place, q_peer, kv_peer, [kv_own] + near, "attend_near_peer")
        for_peer = attend(place, q_peer, kv_peer, far, "attend_far_peer", state_peer, True)
        from_peer = swap(for_peer, "req", 1)
        context = attend(place, q_own, kv_own, far, "attend_far", state_own, True)

    with jax.named_scope("exchange_context"):
        sides = []
        for source in (context, from_peer):
            across = swap(source, "tp", 2)
            sides.append(
                [(source, 0), (swap(source, "tp", 1), 1), (across, 0), (swap(across, "tp", 1), 1)]
            )
        pieces = [sides[h][t] for t in range(4) for h in range(2)]

    with jax.named_scope("mixer"):
        weights = [expand_weight, expand_other, reduce_weight, reduce_other]
        sent, kept, received = [], [], []
        for chunk in range(2):
            s, k = mixer(place, pieces, tokens, mixer_gain, wo, weights, chunk, chunk_rows)
            kept.append(k)
            received.append(swap(s, "tp", 2))

    with jax.named_scope("merge"):
        index = jnp.transpose(merge_index) - req * rows
        earlier = gather(place, index, kept[0], received[0], output_gain)
        own, other = merge(
            place, index, kept[1], received[1], output_gain, earlier, merge_own, merge_other
        )
        other = swap(other, "tp", 1)

    with jax.named_scope("place"):
        capacity = 2 * merge_index.shape[0] // peers
        target = owners[:, 0]
        choose = (target[:, None] == jnp.arange(peers, dtype=jnp.int32)[None, :]).astype(jnp.int32)
        slot = jnp.sum((jnp.cumsum(choose, axis=0) - 1) * choose, axis=1)
        position = (target * capacity + slot)[None, :]
        columns = own.shape[1]
        outgoing = pl.pallas_call(
            place_kernel,
            out_shape=jax.ShapeDtypeStruct((peers * capacity, columns), jnp.bfloat16),
            name="place",
        )(position, own, other)
        outgoing = outgoing.reshape(peers, capacity, columns)
        arrived = lax.all_to_all(outgoing, "req", split_axis=0, concat_axis=0, tiled=True)
    return arrived.reshape(1, peers, capacity, columns)


def solution(mesh):
    placed = (
        P("req", None),
        P("req"),
        P(),
        P(None, None, "tp"),
        P("tp", None),
        P(),
        P(None, "tp"),
        P("tp", None),
        P(),
        P(None, "tp"),
        P("req", None),
        P("req", None),
    )
    return jax.shard_map(
        body, mesh=mesh, in_specs=placed, out_specs=P("req", None, None, "tp"), check_vma=False
    )
```

time: 192 us -> 215 us (1.12); the launches traced: 190 us -> 216 us
  Pallas kernels: 84.3 us -> 103 us
  blocking collectives: 21 us -> 28.2 us
  waiting for transfers between devices: 46.3 us -> 52.7 us
  local copies, waits for them, and re-layouts: 9.53 us -> 4.93 us
    pallas_call x4 -> x6, Pallas kernels: 42.8 us -> 63.7 us  [the longest x5 56.1 us: attend(): pl.pallas_call(functools.partial(attend_kernel, blocks, state is not None...]
    all_to_all x1, blocking collectives: 21 us -> 28.2 us  [body(): lax.all_to_all(outgoing, 'req', split_axis=0, concat_axis=0, tiled=True)]
    ppermute x4, waiting for transfers between devices: 2.35 us -> 7.62 us  [shifted(): return lax.ppermute(block, axis, route)]
    broadcast_in_dim x3 -> x0, local copies, waits for them, and re-layouts: 2.62 us -> none  [the longest x1 1.43 us: body(): attend_gain.astype(jnp.float32)[None, :]]
    unnamed x23 -> x31, local copies, waits for them, and re-layouts: 3.95 us -> 4.71 us
  transfers between devices with their start and end apart: 22 -> 22, of which waited for: 11 -> 10; matrix products, arithmetic and copies ran while one was open for 4% -> 1% of each run, Pallas kernels for 33% -> 39%
where the time goes in v2:
time: 215 us; the launch traced here: 216 us
  Pallas kernels  103 us (48%)
  waiting for transfers between devices  52.7 us (25%)
  blocking collectives  28.2 us (13%)
  starting transfers between devices  24.1 us (11%)
  local copies, waits for them, and re-layouts  4.93 us (2%)
  other arithmetic  2.75 us (1%)
    pallas_call x5, Pallas kernels, attend(): pl.pallas_call(functools.partial(attend_kernel, blocks, state is not None...  56.1 us
    ppermute x18, waiting for transfers between devices, swap(): lax.ppermute(block, axis, [(i, i ^ flip) for i in range(lax.axis_size(axi...  45.1 us
    all_to_all x1, blocking collectives, body(): lax.all_to_all(outgoing, 'req', split_axis=0, concat_axis=0, tiled=True)  28.2 us
    pallas_call x2, Pallas kernels, mixer(): pl.pallas_call(mixer_kernel, grid_spec=pltpu.PrefetchScalarGridSpec(num_s...  23.2 us
    ppermute x18, starting transfers between devices, swap(): lax.ppermute(block, axis, [(i, i ^ flip) for i in range(lax.axis_size(axi...  12.4 us
    ppermute x4, starting transfers between devices, shifted(): return lax.ppermute(block, axis, route)  11.7 us
    pallas_call x1, Pallas kernels, merge(): pl.pallas_call(merge_kernel, grid_spec=pltpu.PrefetchScalarGridSpec(num_s...  9.04 us
    pallas_call x1, Pallas kernels, project(): pl.pallas_call(project_kernel, grid=(rows // step,), in_specs=[pl.BlockSp...  7.67 us
  transfers between devices with their start and end apart: 22, of which 10 were waited for; matrix products, arithmetic and copies ran while one was open for 1% of the time, Pallas kernels for 39%

profile of v2, /device:TPU:0, one launch (start us, length us, event | category | flops | bytes accessed | tf_op | source)
XLA Modules:
  0.0 215.8 jit_solution(7167693947495878152)
XLA Ops:
  0.0 7.7 %project.1 = (bf16[336,1024]{1,0:T(8,128)(2,1)}, bf16[336,1024]{1,0:T(8,128)(2,1)}, bf16[160,1024]{1,0:T(8,128)(2,1)}, bf16[160,1024]{1,0:T(8,128)(2,1)}) custom-call(bf16[1024,1280]{1,0:T(8,128)(2,1)} %refs_8_.3, s32[1,1024]{1,0:T(1,128)} %bitcast.36, bf16[1280]{0:T(1024)(128)(2,1)} %gain_ref.3, bf16[960,1280]{1,0:T(8,128)(2,1)} %bitcast.31), custom_call_target="tpu_custom_call" | custom-call | tf_op jit(solution)/shard_map/project/project/pallas_call | solution.py:81
  7.7 3.0 %collective-permute-start = (bf16[336,1024]{1,0:T(8,128)(2,1)}, bf16[336,1024]{1,0:T(8,128)(2,1)}, u32[]{:S(2)}, u32[]{:S(2)}) collective-permute-start(bf16[336,1024]{1,0:T(8,128)(2,1)} %get-tuple-element.28), channel_id=1, source_target_pairs={{0,4},{4,0},{8,12},{12,8},{16,20},{20,16},{24,28},{28,24},{1,5},{5... | collective-permute-start | bytes 2064392 | tf_op jit(solution)/shard_map/exchange_keys/ppermute | solution.py:24
  10.7 1.5 collective-permute-start.14
  12.2 4.3 %collective-permute-start.3 = (bf16[336,1024]{1,0:T(8,128)(2,1)}, bf16[336,1024]{1,0:T(8,128)(2,1)}, u32[]{:S(2)}, u32[]{:S(2)}) collective-permute-start(bf16[336,1024]{1,0:T(8,128)(2,1)} %get-tuple-element.26.number_ref.refs_0_), channel_id=1, source_target_pairs={{0,8},{4,12},{8,16},{12,20},{16,24},{20,28},{1,9},{5,13},{9,17},{1... | collective-permute-start | bytes 2064392 | tf_op jit(solution)/shard_map/exchange_keys/ppermute | solution.py:30
  16.6 1.3 collective-permute-start.4
  17.9 0.1 collective-permute-start.16
  17.9 8.5 %collective-permute-done.refs_0_.number_ref.refs_1_ = bf16[336,1024]{1,0:T(8,128)(2,1)} collective-permute-done((bf16[336,1024]{1,0:T(8,128)(2,1)}, bf16[336,1024]{1,0:T(8,128)(2,1)}, u32[]{:S(2)}, u32[]{:S(2)}) %collective-permute-start) | collective-permute-done | bytes 688160 | tf_op jit(solution)/shard_map/exchange_keys/ppermute | solution.py:24
  26.4 0.0 collective-permute-start.17
  26.4 0.7 pad_add_fusion.place
  27.1 10.6 %attend_own.1 = (f32[2,2,96,512]{3,2,1,0:T(8,128)}, f32[2,2,512]{2,1,0:T(2,128)}) custom-call(s32[4]{0:T(128)} %pad_add_fusion.place, bf16[160,1024]{1,0:T(8,128)(2,1)} %get-tuple-element.25.q_ref, bf16[336,1024]{1,0:T(8,128)(2,1)} %get-tuple-element.26.number_ref.refs_0_, bf16[336,1024]{1,0:T(8,128)(2,1)} %get-tuple-element.26.number_ref.refs_0_), custom_call_target="tpu_custom_call" | custom-call | flops 1000000000 | bytes 4000000 | tf_op jit(solution)/shard_map/exchange_keys/attend_own/pallas_call | solution.py:245
  37.7 0.0 collective-permute-done.3.refs_1_.refs_2_
  37.7 4.6 %collective-permute-start.1 = (bf16[336,1024]{1,0:T(8,128)(2,1)}, bf16[336,1024]{1,0:T(8,128)(2,1)}, u32[]{:S(2)}, u32[]{:S(2)}) collective-permute-start(bf16[336,1024]{1,0:T(8,128)(2,1)} %collective-permute-done.refs_0_.number_ref.refs_1_), channel_id=1, source_target_pairs={{0,8},{4,12},{8,16},{12,20},{16,24},{20,28},{1,9},{5,13},{9,17},{1... | collective-permute-start | bytes 2064392 | tf_op jit(solution)/shard_map/exchange_keys/ppermute | solution.py:30
  42.3 1.5 collective-permute-start.2
  43.7 0.0 collective-permute-done.14.refs_12_
  43.8 1.6 collective-permute-start.5
  45.3 8.4 %collective-permute-done.5.q_ref = bf16[160,1024]{1,0:T(8,128)(2,1)S(1)} collective-permute-done((bf16[160,1024]{1,0:T(8,128)(2,1)S(1)}, bf16[160,1024]{1,0:T(8,128)(2,1)S(1)}, u32[]{:S(2)}, u32[]{:S(2)}) %collective-permute-start.5) | collective-permute-done | bytes 327712 | tf_op jit(solution)/shard_map/exchange_keys/ppermute | solution.py:24
  53.7 0.7 copy-done.14
  54.4 2.7 %collective-permute-done.1.refs_0_ = bf16[336,1024]{1,0:T(8,128)(2,1)} collective-permute-done((bf16[336,1024]{1,0:T(8,128)(2,1)}, bf16[336,1024]{1,0:T(8,128)(2,1)}, u32[]{:S(2)}, u32[]{:S(2)}) %collective-permute-start.1) | collective-permute-done | bytes 688160 | tf_op jit(solution)/shard_map/exchange_keys/ppermute | solution.py:30
  57.1 0.0 collective-permute-start.20
  57.1 5.0 %collective-permute-done.2.refs_1_ = bf16[336,1024]{1,0:T(8,128)(2,1)} collective-permute-done((bf16[336,1024]{1,0:T(8,128)(2,1)}, bf16[336,1024]{1,0:T(8,128)(2,1)}, u32[]{:S(2)}, u32[]{:S(2)}) %collective-permute-start.2) | collective-permute-done | bytes 688160 | tf_op jit(solution)/shard_map/exchange_keys/ppermute | solution.py:30
  62.0 0.0 collective-permute-start.15
  62.0 23.0 %attend_near_peer.1 = (f32[2,2,96,512]{3,2,1,0:T(8,128)}, f32[2,2,512]{2,1,0:T(2,128)}) custom-call(s32[4]{0:T(128)} %pad_add_fusion.place, bf16[160,1024]{1,0:T(8,128)(2,1)} %copy-done.14, bf16[336,1024]{1,0:T(8,128)(2,1)} %collective-permute-done.refs_0_.number_ref.refs_1_, bf16[336,1024]{1,0:T(8,128)(2,1)} %get-tuple-element.26.number_ref.refs_0_, ...), custom_call_target="tpu_custom_call" | custom-call | flops 4000000000 | bytes 4000000 | tf_op jit(solution)/shard_map/attention/attend_near_peer/pallas_call | solution.py:245
  85.0 6.0 %attend_far_peer.1 = bf16[2,160,512]{2,1,0:T(8,128)(2,1)} custom-call(s32[4]{0:T(128)} %pad_add_fusion.place, bf16[160,1024]{1,0:T(8,128)(2,1)} %copy-done.14, bf16[336,1024]{1,0:T(8,128)(2,1)} %collective-permute-done.refs_0_.number_ref.refs_1_, bf16[336,1024]{1,0:T(8,128)(2,1)} %collective-permute-done.1.refs_0_, ...), custom_call_target="tpu_custom_call" | custom-call | flops 2000000000 | bytes 4000000 | tf_op jit(solution)/shard_map/attention/attend_far_peer/pallas_call | solution.py:245
  91.1 0.0 collective-permute-done.13.refs_11_
  91.1 0.1 collective-permute-start.6
  91.1 12.0 %attend_near.1 = (f32[2,2,96,512]{3,2,1,0:T(8,128)}, f32[2,2,512]{2,1,0:T(2,128)}) custom-call(s32[4]{0:T(128)} %pad_add_fusion.place, bf16[160,1024]{1,0:T(8,128)(2,1)} %get-tuple-element.25.q_ref, bf16[336,1024]{1,0:T(8,128)(2,1)} %get-tuple-element.26.number_ref.refs_0_, bf16[336,1024]{1,0:T(8,128)(2,1)} %collective-permute-done.refs_0_.number_ref.refs_1_, ...), custom_call_target="tpu_custom_call" | custom-call | flops 3000000000 | bytes 4000000 | tf_op jit(solution)/shard_map/attention/attend_near/pallas_call | solution.py:245
  103.2 4.5 %attend_far.1.refs_0_ = bf16[2,160,512]{2,1,0:T(8,128)(2,1)} custom-call(s32[4]{0:T(128)} %pad_add_fusion.place, bf16[160,1024]{1,0:T(8,128)(2,1)} %get-tuple-element.25.q_ref, bf16[336,1024]{1,0:T(8,128)(2,1)} %get-tuple-element.26.number_ref.refs_0_, bf16[336,1024]{1,0:T(8,128)(2,1)} %collective-permute-done.1.refs_0_, ...), custom_call_target="tpu_custom_call" | custom-call | flops 2000000000 | bytes 4000000 | tf_op jit(solution)/shard_map/attention/attend_far/pallas_call | solution.py:245
  107.6 0.0 collective-permute-done.15.refs_13_
  107.6 0.6 collective-permute-start.7
  108.2 0.0 collective-permute-done.6.refs_1_
  108.2 1.5 collective-permute-start.9
  109.7 0.0 collective-permute-done.7.refs_2_
  109.7 0.3 collective-permute-start.8
  110.0 8.1 %collective-permute-done.9.refs_4_ = bf16[2,160,512]{2,1,0:T(8,128)(2,1)S(1)} collective-permute-done((bf16[2,160,512]{2,1,0:T(8,128)(2,1)}, bf16[2,160,512]{2,1,0:T(8,128)(2,1)S(1)}, u32[]{:S(2)}, u32[]{:S(2)}) %collective-permute-start.9) | collective-permute-done | bytes 327712 | tf_op jit(solution)/shard_map/exchange_context/ppermute | solution.py:24
  118.1 1.5 collective-permute-start.10
  119.6 0.0 collective-permute-done.8.refs_3_
  119.7 7.3 %collective-permute-done.10.refs_5_ = bf16[2,160,512]{2,1,0:T(8,128)(2,1)S(1)} collective-permute-done((bf16[2,160,512]{2,1,0:T(8,128)(2,1)S(1)}, bf16[2,160,512]{2,1,0:T(8,128)(2,1)S(1)}, u32[]{:S(2)}, u32[]{:S(2)}) %collective-permute-start.10) | collective-permute-done | bytes 327712 | tf_op jit(solution)/shard_map/exchange_context/ppermute | solution.py:24
  127.0 0.0 collective-permute-done.11.refs_6_
  127.0 1.6 collective-permute-done.12.refs_7_
  128.7 0.7 copy-done.7
  129.4 11.6 %mixer.3 = (bf16[256,1280]{1,0:T(8,128)(2,1)}, f32[256,1280]{1,0:T(8,128)}) custom-call(s32[4]{0:T(128)} %pad_add_fusion.place, bf16[2,160,512]{2,1,0:T(8,128)(2,1)} %attend_far.1.refs_0_, bf16[2,160,512]{2,1,0:T(8,128)(2,1)} %copy-done.1, bf16[2,160,512]{2,1,0:T(8,128)(2,1)} %copy-done.2, bf16[2,160,512]{2,1,0:T(8,128)(2,1)} %copy-done.4, ...), custom_call_target="tpu_custom_call" | custom-call | flops 5000000000 | bytes 20000000 | tf_op jit(solution)/shard_map/mixer/mixer/pallas_call | solution.py:320
  141.0 0.0 copy-start.11
  141.0 0.0 copy-start.12
  141.0 1.6 collective-permute-start.19
  142.6 11.6 %mixer.2 = (bf16[256,1280]{1,0:T(8,128)(2,1)}, f32[256,1280]{1,0:T(8,128)}) custom-call(s32[4]{0:T(128)} %pad_add_fusion.place, bf16[2,160,512]{2,1,0:T(8,128)(2,1)} %attend_far.1.refs_0_, bf16[2,160,512]{2,1,0:T(8,128)(2,1)} %copy-done.1, bf16[2,160,512]{2,1,0:T(8,128)(2,1)} %copy-done.2, bf16[2,160,512]{2,1,0:T(8,128)(2,1)} %copy-done.4, ...), custom_call_target="tpu_custom_call" | custom-call | flops 5000000000 | bytes 20000000 | tf_op jit(solution)/shard_map/mixer/mixer/pallas_call | solution.py:320
  154.2 0.6 collective-permute-start.18
  154.7 0.8 reduce-window.6
  155.5 0.2 slice_reduce_fusion
  155.8 0.6 subtract_bitcast_fusion.index_ref
  156.4 2.5 %collective-permute-done.19.received = bf16[256,1280]{1,0:T(8,128)(2,1)S(1)} collective-permute-done((bf16[256,1280]{1,0:T(8,128)(2,1)}, bf16[256,1280]{1,0:T(8,128)(2,1)S(1)}, u32[]{:S(2)}, u32[]{:S(2)}) %collective-permute-start.19) | collective-permute-done | bytes 655392 | tf_op jit(solution)/shard_map/mixer/ppermute | solution.py:24
  158.9 0.9 copy-done.9
  159.8 4.9 %gather.1.refs_0_ = bf16[4,256,1280]{2,1,0:T(8,128)(2,1)} custom-call(s32[4]{0:T(128)} %pad_add_fusion.place, s32[4,256]{1,0:T(4,128)} %subtract_bitcast_fusion.index_ref, f32[256,1280]{1,0:T(8,128)} %get-tuple-element.41.kept, bf16[256,1280]{1,0:T(8,128)(2,1)} %copy-done.9, bf16[1280]{0:T(1024)(128)(2,1)} %gain_ref.5), custom_call_target="tpu_custom_call" | custom-call | flops 1000000000 | bytes 5000000 | tf_op jit(solution)/shard_map/merge/gather/pallas_call | solution.py:371
  164.6 0.0 collective-permute-done.20.refs_2_
  164.6 7.5 %collective-permute-done.18.received = bf16[256,1280]{1,0:T(8,128)(2,1)S(1)} collective-permute-done((bf16[256,1280]{1,0:T(8,128)(2,1)}, bf16[256,1280]{1,0:T(8,128)(2,1)S(1)}, u32[]{:S(2)}, u32[]{:S(2)}) %collective-permute-start.18) | collective-permute-done | bytes 655392 | tf_op jit(solution)/shard_map/mixer/ppermute | solution.py:24
  172.1 0.8 copy-done.8
  172.9 9.0 %merge.1 = (f32[256,320]{1,0:T(8,128)}, f32[256,320]{1,0:T(8,128)}) custom-call(s32[4]{0:T(128)} %pad_add_fusion.place, s32[4,256]{1,0:T(4,128)} %subtract_bitcast_fusion.index_ref, f32[256,1280]{1,0:T(8,128)} %get-tuple-element.39.kept, bf16[256,1280]{1,0:T(8,128)(2,1)} %copy-done.8, bf16[1280]{0:T(1024)(128)(2,1)} %gain_ref.5, ...), custom_call_target="tpu_custom_call" | custom-call | flops 3000000000 | bytes 12000000 | tf_op jit(solution)/shard_map/merge/merge/pallas_call | solution.py:420
  182.0 0.1 collective-permute-start.21
  182.1 0.1 fusion
  182.2 0.5 bitcast_add_fusion.position
  182.7 1.3 collective-permute-done.21.received
  184.0 0.8 copy-done.10
  184.7 2.2 %place.1 = bf16[512,320]{1,0:T(8,128)(2,1)} custom-call(s32[1,256]{1,0:T(1,128)} %bitcast_add_fusion.position, f32[256,320]{1,0:T(8,128)} %get-tuple-element.43.own, f32[256,320]{1,0:T(8,128)} %copy-done.10), custom_call_target="tpu_custom_call" | custom-call | tf_op jit(solution)/shard_map/place/place/pallas_call | solution.py:539
  186.9 28.2 %all_to_all.5 = bf16[8,64,320]{2,1,0:T(8,128)(2,1)S(1)} all-to-all(bf16[8,64,320]{2,1,0:T(8,128)(2,1)} %bitcast.33), channel_id=1, replica_groups=mesh['req'=8,'tp'=4] {'req'}, dimensions={0} | all-to-all | bytes 655360 | tf_op jit(solution)/shard_map/place/all_to_all | solution.py:545
  215.1 0.7 copy.14
  (32 shorter events, 0.1 us)
Async XLA Ops:
  0.0 17.8 %copy-start = (bf16[1280,1280]{1,0:T(8,128)(2,1)S(1)}, bf16[1280,1280]{1,0:T(8,128)(2,1)}, u32[]{:S(2)}) copy-start(bf16[1280,1280]{1,0:T(8,128)(2,1)} %refs_14_.3) | copy-start | bytes 9830404
  7.7 18.8 %collective-permute-start = (bf16[336,1024]{1,0:T(8,128)(2,1)}, bf16[336,1024]{1,0:T(8,128)(2,1)}, u32[]{:S(2)}, u32[]{:S(2)}) collective-permute-start(bf16[336,1024]{1,0:T(8,128)(2,1)} %get-tuple-element.28), channel_id=1, source_target_pairs={{0,4},{4,0},{8,12},{12,8},{16,20},{20,16},{24,28},{28,24},{1,5},{5... | collective-permute-start | bytes 2064392 | tf_op jit(solution)/shard_map/exchange_keys/ppermute | solution.py:24
  10.7 33.1 %collective-permute-start.14 = (bf16[2,160,1280]{2,1,0:T(8,128)(2,1)}, bf16[2,160,1280]{2,1,0:T(8,128)(2,1)}, u32[]{:S(2)}, u32[]{:S(2)}) collective-permute-start(bf16[2,160,1280]{2,1,0:T(8,128)(2,1)} %bitcast.27), channel_id=1, source_target_pairs={{0,2},{1,3},{2,0},{3,1},{4,6},{5,7},{6,4},{7,5},{8,10},{9,11},{10,... | collective-permute-start | bytes 2457608 | tf_op jit(solution)/shard_map/weights/ppermute | solution.py:24
  12.2 25.5 %collective-permute-start.3 = (bf16[336,1024]{1,0:T(8,128)(2,1)}, bf16[336,1024]{1,0:T(8,128)(2,1)}, u32[]{:S(2)}, u32[]{:S(2)}) collective-permute-start(bf16[336,1024]{1,0:T(8,128)(2,1)} %get-tuple-element.26.number_ref.refs_0_), channel_id=1, source_target_pairs={{0,8},{4,12},{8,16},{12,20},{16,24},{20,28},{1,9},{5,13},{9,17},{1... | collective-permute-start | bytes 2064392 | tf_op jit(solution)/shard_map/exchange_keys/ppermute | solution.py:30
  16.6 25.7 %collective-permute-start.4 = (bf16[336,1024]{1,0:T(8,128)(2,1)}, bf16[336,1024]{1,0:T(8,128)(2,1)}, u32[]{:S(2)}, u32[]{:S(2)}) collective-permute-start(bf16[336,1024]{1,0:T(8,128)(2,1)} %get-tuple-element.26.number_ref.refs_0_), channel_id=1, source_target_pairs={{8,0},{12,4},{16,8},{20,12},{24,16},{28,20},{9,1},{13,5},{17,9},{2... | collective-permute-start | bytes 2064392 | tf_op jit(solution)/shard_map/exchange_keys/ppermute | solution.py:30
  17.9 110.8 %collective-permute-start.16 = (bf16[1280,1280]{1,0:T(8,128)(2,1)S(1)}, bf16[1280,1280]{1,0:T(8,128)(2,1)}, u32[]{:S(2)}, u32[]{:S(2)}) collective-permute-start(bf16[1280,1280]{1,0:T(8,128)(2,1)S(1)} %copy-done), channel_id=1, source_target_pairs={{0,1},{1,0},{2,3},{3,2},{4,5},{5,4},{6,7},{7,6},{8,9},{9,8},{10,11... | collective-permute-start | bytes 9830408 | tf_op jit(solution)/shard_map/weights/ppermute | solution.py:24
  26.4 102.9 %collective-permute-start.17 = (bf16[1280,1280]{1,0:T(8,128)(2,1)}, bf16[1280,1280]{1,0:T(8,128)(2,1)}, u32[]{:S(2)}, u32[]{:S(2)}) collective-permute-start(bf16[1280,1280]{1,0:T(8,128)(2,1)} %refs_16_.3), channel_id=1, source_target_pairs={{0,1},{1,0},{2,3},{3,2},{4,5},{5,4},{6,7},{7,6},{8,9},{9,8},{10,11... | collective-permute-start | bytes 9830408 | tf_op jit(solution)/shard_map/weights/ppermute | solution.py:24
  26.4 17.3 %copy-start.13 = (bf16[160,1024]{1,0:T(8,128)(2,1)S(1)}, bf16[160,1024]{1,0:T(8,128)(2,1)}, u32[]{:S(2)}) copy-start(bf16[160,1024]{1,0:T(8,128)(2,1)} %get-tuple-element.36) | copy-start | bytes 983044
  37.7 19.4 %collective-permute-start.1 = (bf16[336,1024]{1,0:T(8,128)(2,1)}, bf16[336,1024]{1,0:T(8,128)(2,1)}, u32[]{:S(2)}, u32[]{:S(2)}) collective-permute-start(bf16[336,1024]{1,0:T(8,128)(2,1)} %collective-permute-done.refs_0_.number_ref.refs_1_), channel_id=1, source_target_pairs={{0,8},{4,12},{8,16},{12,20},{16,24},{20,28},{1,9},{5,13},{9,17},{1... | collective-permute-start | bytes 2064392 | tf_op jit(solution)/shard_map/exchange_keys/ppermute | solution.py:30
  42.3 19.8 %collective-permute-start.2 = (bf16[336,1024]{1,0:T(8,128)(2,1)}, bf16[336,1024]{1,0:T(8,128)(2,1)}, u32[]{:S(2)}, u32[]{:S(2)}) collective-permute-start(bf16[336,1024]{1,0:T(8,128)(2,1)} %collective-permute-done.refs_0_.number_ref.refs_1_), channel_id=1, source_target_pairs={{8,0},{12,4},{16,8},{20,12},{24,16},{28,20},{9,1},{13,5},{17,9},{2... | collective-permute-start | bytes 2064392 | tf_op jit(solution)/shard_map/exchange_keys/ppermute | solution.py:30
  43.8 9.9 %collective-permute-start.5 = (bf16[160,1024]{1,0:T(8,128)(2,1)S(1)}, bf16[160,1024]{1,0:T(8,128)(2,1)S(1)}, u32[]{:S(2)}, u32[]{:S(2)}) collective-permute-start(bf16[160,1024]{1,0:T(8,128)(2,1)S(1)} %copy-done.13), channel_id=1, source_target_pairs={{0,4},{4,0},{8,12},{12,8},{16,20},{20,16},{24,28},{28,24},{1,5},{5... | collective-permute-start | bytes 983048 | tf_op jit(solution)/shard_map/exchange_keys/ppermute | solution.py:24
  53.7 0.7 copy-start.14
  54.4 36.6 %collective-permute-start.13 = (bf16[2,160,1280]{2,1,0:T(8,128)(2,1)}, bf16[2,160,1280]{2,1,0:T(8,128)(2,1)}, u32[]{:S(2)}, u32[]{:S(2)}) collective-permute-start(bf16[2,160,1280]{2,1,0:T(8,128)(2,1)} %bitcast.28), channel_id=1, source_target_pairs={{0,1},{1,0},{2,3},{3,2},{4,5},{5,4},{6,7},{7,6},{8,9},{9,8},{10,11... | collective-permute-start | bytes 2457608 | tf_op jit(solution)/shard_map/weights/ppermute | solution.py:24
  57.1 107.5 %collective-permute-start.20 = (bf16[320,5120]{1,0:T(8,128)(2,1)}, bf16[320,5120]{1,0:T(8,128)(2,1)}, u32[]{:S(2)}, u32[]{:S(2)}) collective-permute-start(bf16[320,5120]{1,0:T(8,128)(2,1)} %bitcast.25), channel_id=1, source_target_pairs={{0,1},{1,0},{2,3},{3,2},{4,5},{5,4},{6,7},{7,6},{8,9},{9,8},{10,11... | collective-permute-start | bytes 9830408 | tf_op jit(solution)/shard_map/weights/ppermute | solution.py:24
  62.0 45.6 %collective-permute-start.15 = (bf16[2,160,1280]{2,1,0:T(8,128)(2,1)}, bf16[2,160,1280]{2,1,0:T(8,128)(2,1)}, u32[]{:S(2)}, u32[]{:S(2)}) collective-permute-start(bf16[2,160,1280]{2,1,0:T(8,128)(2,1)} %collective-permute-done.14.refs_12_), channel_id=1, source_target_pairs={{0,1},{1,0},{2,3},{3,2},{4,5},{5,4},{6,7},{7,6},{8,9},{9,8},{10,11... | collective-permute-start | bytes 2457608 | tf_op jit(solution)/shard_map/weights/ppermute | solution.py:24
  91.1 17.1 %collective-permute-start.6 = (bf16[2,160,512]{2,1,0:T(8,128)(2,1)}, bf16[2,160,512]{2,1,0:T(8,128)(2,1)S(1)}, u32[]{:S(2)}, u32[]{:S(2)}) collective-permute-start(bf16[2,160,512]{2,1,0:T(8,128)(2,1)} %attend_far_peer.1), channel_id=1, source_target_pairs={{0,4},{4,0},{8,12},{12,8},{16,20},{20,16},{24,28},{28,24},{1,5},{5... | collective-permute-start | bytes 983048 | tf_op jit(solution)/shard_map/attention/ppermute | solution.py:24
  107.6 2.1 collective-permute-start.7
  108.2 21.2 %copy-start.1 = (bf16[2,160,512]{2,1,0:T(8,128)(2,1)}, bf16[2,160,512]{2,1,0:T(8,128)(2,1)S(1)}, u32[]{:S(2)}) copy-start(bf16[2,160,512]{2,1,0:T(8,128)(2,1)S(1)} %collective-permute-done.6.refs_1_) | copy-start | bytes 983044
  108.2 9.9 %collective-permute-start.9 = (bf16[2,160,512]{2,1,0:T(8,128)(2,1)}, bf16[2,160,512]{2,1,0:T(8,128)(2,1)S(1)}, u32[]{:S(2)}, u32[]{:S(2)}) collective-permute-start(bf16[2,160,512]{2,1,0:T(8,128)(2,1)} %attend_far.1.refs_0_), channel_id=1, source_target_pairs={{0,2},{1,3},{2,0},{3,1},{4,6},{5,7},{6,4},{7,5},{8,10},{9,11},{10,... | collective-permute-start | bytes 983048 | tf_op jit(solution)/shard_map/exchange_context/ppermute | solution.py:24
  109.7 18.9 %copy-start.2 = (bf16[2,160,512]{2,1,0:T(8,128)(2,1)}, bf16[2,160,512]{2,1,0:T(8,128)(2,1)S(1)}, u32[]{:S(2)}) copy-start(bf16[2,160,512]{2,1,0:T(8,128)(2,1)S(1)} %collective-permute-done.7.refs_2_) | copy-start | bytes 983044
  109.7 9.9 %collective-permute-start.8 = (bf16[2,160,512]{2,1,0:T(8,128)(2,1)S(1)}, bf16[2,160,512]{2,1,0:T(8,128)(2,1)S(1)}, u32[]{:S(2)}, u32[]{:S(2)}) collective-permute-start(bf16[2,160,512]{2,1,0:T(8,128)(2,1)S(1)} %collective-permute-done.6.refs_1_), channel_id=1, source_target_pairs={{0,1},{1,0},{2,3},{3,2},{4,5},{5,4},{6,7},{7,6},{8,9},{9,8},{10,11... | collective-permute-start | bytes 983048 | tf_op jit(solution)/shard_map/exchange_context/ppermute | solution.py:24
  118.1 10.5 %copy-start.3 = (bf16[2,160,512]{2,1,0:T(8,128)(2,1)}, bf16[2,160,512]{2,1,0:T(8,128)(2,1)S(1)}, u32[]{:S(2)}) copy-start(bf16[2,160,512]{2,1,0:T(8,128)(2,1)S(1)} %collective-permute-done.9.refs_4_) | copy-start | bytes 983044
  118.1 8.9 %collective-permute-start.10 = (bf16[2,160,512]{2,1,0:T(8,128)(2,1)S(1)}, bf16[2,160,512]{2,1,0:T(8,128)(2,1)S(1)}, u32[]{:S(2)}, u32[]{:S(2)}) collective-permute-start(bf16[2,160,512]{2,1,0:T(8,128)(2,1)S(1)} %collective-permute-done.6.refs_1_), channel_id=1, source_target_pairs={{0,2},{1,3},{2,0},{3,1},{4,6},{5,7},{6,4},{7,5},{8,10},{9,11},{10,... | collective-permute-start | bytes 983048 | tf_op jit(solution)/shard_map/exchange_context/ppermute | solution.py:24
  119.6 9.0 %copy-start.4 = (bf16[2,160,512]{2,1,0:T(8,128)(2,1)}, bf16[2,160,512]{2,1,0:T(8,128)(2,1)S(1)}, u32[]{:S(2)}) copy-start(bf16[2,160,512]{2,1,0:T(8,128)(2,1)S(1)} %collective-permute-done.8.refs_3_) | copy-start | bytes 983044
  119.7 7.4 %collective-permute-start.11 = (bf16[2,160,512]{2,1,0:T(8,128)(2,1)S(1)}, bf16[2,160,512]{2,1,0:T(8,128)(2,1)S(1)}, u32[]{:S(2)}, u32[]{:S(2)}) collective-permute-start(bf16[2,160,512]{2,1,0:T(8,128)(2,1)S(1)} %collective-permute-done.9.refs_4_), channel_id=1, source_target_pairs={{0,1},{1,0},{2,3},{3,2},{4,5},{5,4},{6,7},{7,6},{8,9},{9,8},{10,11... | collective-permute-start | bytes 983048 | tf_op jit(solution)/shard_map/exchange_context/ppermute | solution.py:24
  127.0 1.7 copy-start.5
  127.0 1.6 collective-permute-start.12
  127.0 1.7 copy-start.6
  128.6 0.7 copy-start.7
  141.0 13.8 %copy-start.11 = (s32[256,1]{0,1:T(1,128)S(1)}, s32[256,1]{0,1:T(1,128)}, u32[]{:S(2)}) copy-start(s32[256,1]{0,1:T(1,128)} %param.23) | copy-start | bytes 3076
  141.0 14.8 %copy-start.12 = (s32[256,4]{0,1:T(4,128)S(1)}, s32[256,4]{0,1:T(4,128)}, u32[]{:S(2)}) copy-start(s32[256,4]{0,1:T(4,128)} %param.22) | copy-start | bytes 12292
  141.0 17.9 %collective-permute-start.19 = (bf16[256,1280]{1,0:T(8,128)(2,1)}, bf16[256,1280]{1,0:T(8,128)(2,1)S(1)}, u32[]{:S(2)}, u32[]{:S(2)}) collective-permute-start(bf16[256,1280]{1,0:T(8,128)(2,1)} %get-tuple-element.42), channel_id=1, source_target_pairs={{0,2},{1,3},{2,0},{3,1},{4,6},{5,7},{6,4},{7,5},{8,10},{9,11},{10,... | collective-permute-start | bytes 1966088 | tf_op jit(solution)/shard_map/mixer/ppermute | solution.py:24
  154.2 17.9 %collective-permute-start.18 = (bf16[256,1280]{1,0:T(8,128)(2,1)}, bf16[256,1280]{1,0:T(8,128)(2,1)S(1)}, u32[]{:S(2)}, u32[]{:S(2)}) collective-permute-start(bf16[256,1280]{1,0:T(8,128)(2,1)} %get-tuple-element.40), channel_id=1, source_target_pairs={{0,2},{1,3},{2,0},{3,1},{4,6},{5,7},{6,4},{7,5},{8,10},{9,11},{10,... | collective-permute-start | bytes 1966088 | tf_op jit(solution)/shard_map/mixer/ppermute | solution.py:24
  158.9 0.9 copy-start.9
  172.1 0.8 copy-start.8
  182.0 2.0 collective-permute-start.21
  184.0 0.8 copy-start.10
